TPU v7x, 32 devices: a whole 2x2x4 slice. The times are simulated.
32 devices in a mesh: dp: 8 (over y, x, core), seq: 4 (over z).
Axes of the slice: x: 2, y: 2, z: 4, core: 2. Of those that a mesh axis runs over, the one named last changes fastest.
Arguments:
- queries: bfloat16 [16384, 1536], P(('dp', 'seq')), may hold values from -8 to 8
- keys: bfloat16 [16384, 1536], P(('dp', 'seq')), may hold values from -8 to 8
- values: bfloat16 [16384, 1536], P(('dp', 'seq')), may hold values from -6 to 6
- grad_out: bfloat16 [16384, 1536], P(('dp', 'seq')), may hold values from -6 to 6
- out_weight: bfloat16 [1536, 1536], P('dp'), may hold values from -0.15625 to 0.15625
- lengths: int32 [8], P('dp'), may hold values from 256 to 2048, as said below
Outputs:
- grad_queries: bfloat16 [16384, 1536], P(('dp', 'seq'))
- grad_keys: bfloat16 [16384, 1536], P(('dp', 'seq'))
- grad_values: bfloat16 [16384, 1536], P(('dp', 'seq'))
- grad_weight: float32 [1536, 1536], P(('dp', 'seq'))
Inputs may be any that keep to these rules, and one draw needn't show every extreme that they name: `lengths`: every draw holds one stretch of 2048 valid bytes and one of 256.
All inputs are finite; a program needn't handle non-finite values.
Results may differ from a plain program's by a relative error of at most 0.0058.
Values may be sent and summed in bfloat16 or wider, within the bound.
A program may use at most 192 MiB of HBM per device.

v0:
```python
import jax
import jax.numpy as jnp
from jax import lax
from jax.sharding import PartitionSpec as P

HEADS = 12
HEAD_DIM = 128
WINDOW = 512


def extended(block, sides, width):
    for axis, dim in sides:
        count = lax.axis_size(axis)
        forward = [(i, i + 1) for i in range(count - 1)]
        backward = [(target, source) for source, target in forward]
        low = lax.ppermute(
            lax.slice_in_dim(block, block.shape[dim] - width, None, axis=dim), axis, forward
        )
        high = lax.ppermute(lax.slice_in_dim(block, 0, width, axis=dim), axis, backward)
        block = jnp.concatenate([low, block, high], axis=dim)
    return block


def passed_along(value, axis, by):
    devices = lax.axis_size(axis)
    pairs = [(i, i + by) for i in range(devices) if 0 <= i + by < devices]
    return lax.ppermute(value, axis, pairs)


def window_backward(query_block, key_window, value_window, grad_block, query_pos, key_pos, length):
    half_window = WINDOW // 2
    inv_root = HEAD_DIM ** (-0.5)
    offset = key_pos[None, :] - query_pos[:, None]
    allowed = (offset >= -half_window) & (offset < half_window)
    allowed = (
        allowed
        & (key_pos[None, :] >= 0)
        & (key_pos[None, :] < length)
        & (query_pos[:, None] < length)
    )

    def split_heads(matrix):
        return matrix.reshape(matrix.shape[0], HEADS, HEAD_DIM).transpose(1, 0, 2)

    def join_heads(stacked):
        return stacked.transpose(1, 0, 2).reshape(stacked.shape[1], HEADS * HEAD_DIM)

    def one_head(operands):
        query_head, key_head, value_head, grad_head = operands
        scores = (
            lax.dot_general(
                query_head, key_head, (((1,), (1,)), ((), ())), preferred_element_type=jnp.float32
            )
            * inv_root
        )
        scores = jnp.where(allowed, scores, -1e30)
        row_max = jnp.max(scores, axis=1, keepdims=True)
        expo = jnp.where(allowed, jnp.exp(scores - row_max), 0.0)
        row_total = jnp.maximum(jnp.sum(expo, axis=1, keepdims=True), 1.0)
        probability = expo / row_total
        probability_b = probability.astype(jnp.bfloat16)
        attended_head = jnp.dot(probability_b, value_head, preferred_element_type=jnp.float32)
        grad_probs = lax.dot_general(
            grad_head, value_head, (((1,), (1,)), ((), ())), preferred_element_type=jnp.float32
        )
        row_delta = jnp.sum(probability * grad_probs, axis=1, keepdims=True)
        grad_scores = (probability * (grad_probs - row_delta) * inv_root).astype(jnp.bfloat16)
        grad_query = jnp.dot(grad_scores, key_head, preferred_element_type=jnp.float32)
        grad_key = lax.dot_general(
            grad_scores, query_head, (((0,), (0,)), ((), ())), preferred_element_type=jnp.float32
        )
        grad_value = lax.dot_general(
            probability_b, grad_head, (((0,), (0,)), ((), ())), preferred_element_type=jnp.float32
        )
        return (attended_head, grad_query, grad_key, grad_value)

    outputs = lax.map(
        one_head,
        (
            split_heads(query_block),
            split_heads(key_window),
            split_heads(value_window),
            split_heads(grad_block),
        ),
    )
    attended_heads, grad_query, grad_key, grad_value = outputs
    return (
        join_heads(attended_heads).astype(jnp.bfloat16),
        join_heads(grad_query),
        join_heads(grad_key),
        join_heads(grad_value),
    )


def shards(queries, keys, values, grad_out, out_weight, lengths):
    tok_rows, feat_width = queries.shape
    half_window = WINDOW // 2
    window_rows = tok_rows + 2 * half_window
    seq_index = lax.axis_index("seq")
    first_row = seq_index * tok_rows
    length = lengths[0]
    grad_mixed = jnp.dot(
        grad_out,
        lax.all_gather(out_weight, "dp", axis=0, tiled=True),
        preferred_element_type=jnp.float32,
    ).astype(jnp.bfloat16)
    stacked = jnp.stack([keys, values])
    padded = extended(stacked, (("seq", 1),), half_window)
    query_pos = first_row + jnp.arange(tok_rows, dtype=jnp.int32)
    key_pos = first_row - half_window + jnp.arange(window_rows, dtype=jnp.int32)
    attended, grad_query, grad_key, grad_value = window_backward(
        queries, padded[0], padded[1], grad_mixed, query_pos, key_pos, length
    )
    rim_grads = jnp.stack([grad_key, grad_value])
    from_right = passed_along(rim_grads[:, :half_window], "seq", -1)
    from_left = passed_along(rim_grads[:, tok_rows + half_window :], "seq", 1)
    own_grads = rim_grads[:, half_window : half_window + tok_rows]
    own_grads = own_grads.at[:, :half_window].add(from_left)
    own_grads = own_grads.at[:, tok_rows - half_window :].add(from_right)
    partial_grad = lax.psum_scatter(
        lax.dot_general(
            grad_out, attended, (((0,), (0,)), ((), ())), preferred_element_type=jnp.float32
        ),
        "dp",
        scatter_dimension=0,
        tiled=True,
    )
    weight_grad = lax.psum_scatter(partial_grad, "seq", scatter_dimension=0, tiled=True)
    return (
        grad_query.astype(jnp.bfloat16),
        own_grads[0].astype(jnp.bfloat16),
        own_grads[1].astype(jnp.bfloat16),
        weight_grad,
    )


def solution(mesh):
    in_specs = (
        P(("dp", "seq"), None),
        P(("dp", "seq"), None),
        P(("dp", "seq"), None),
        P(("dp", "seq"), None),
        P("dp", None),
        P("dp"),
    )
    out_specs = (
        P(("dp", "seq"), None),
        P(("dp", "seq"), None),
        P(("dp", "seq"), None),
        P(("dp", "seq"), None),
    )
    return jax.shard_map(shards, mesh=mesh, in_specs=in_specs, out_specs=out_specs, check_vma=False)
```

profile of v0, /device:TPU:0, one launch (start us, length us, event | category | flops | bytes accessed | tf_op | source)
XLA Modules:
  0.0 487.3 jit_solution(13431964834411691836)
XLA Ops:
  9.7 2.6 copy.33
  12.3 3.2 fusion.47
  15.5 6.2 %collective-permute-start = (bf16[2,256,1536]{1,2,0:T(8,128)(2,1)}, bf16[2,256,1536]{1,2,0:T(8,128)(2,1)}, u32[]{:S(2)}, u32[]{:S(2)}) collective-permute-start(bf16[2,256,1536]{1,2,0:T(8,128)(2,1)} %get-tuple-element.200), channel_id=1, source_target_pairs={{0,1},{1,2},{2,3},{4,5},{5,6},{6,7},{8,9},{9,10},{10,11},{12,13},{... | collective-permute-start | bytes 4718600 | tf_op jit(solution)/shard_map/ppermute | solution.py:16
  23.7 2.6 copy.31
  26.3 28.1 %collective-permute-done = bf16[2,256,1536]{1,2,0:T(8,128)(2,1)} collective-permute-done((bf16[2,256,1536]{1,2,0:T(8,128)(2,1)}, bf16[2,256,1536]{1,2,0:T(8,128)(2,1)}, u32[]{:S(2)}, u32[]{:S(2)}) %collective-permute-start) | collective-permute-done | bytes 1572896 | tf_op jit(solution)/shard_map/ppermute | solution.py:16
  54.4 5.3 %collective-permute-done.1 = bf16[2,256,1536]{1,2,0:T(8,128)(2,1)} collective-permute-done((bf16[2,256,1536]{1,2,0:T(8,128)(2,1)}, bf16[2,256,1536]{1,2,0:T(8,128)(2,1)}, u32[]{:S(2)}, u32[]{:S(2)}) %collective-permute-start.1) | collective-permute-done | bytes 1572896 | tf_op jit(solution)/shard_map/ppermute | solution.py:19
  59.7 3.3 pad_maximum_fusion
  63.1 3.4 fusion.50
  66.5 6.0 %convolution_convert_fusion = bf16[512,1536]{1,0:T(8,128)(2,1)} fusion(bf16[512,1536]{1,0:T(8,128)(2,1)S(1)} %copy-done, bf16[1536,1536]{1,0:T(8,128)(2,1)} %all-gather.2.cloned.1.call-done), kind=kOutput, calls=%fused_computation.67 | convolution fusion | flops 2416705536 | bytes 7864320 | tf_op jit(solution)/shard_map/dot_general | solution.py:102
  74.2 210.5 %while.19 = (s32[]{:T(128)}, bf16[12,512,128]{1,2,0:T(8,128)(2,1)}, bf16[12,512,128]{1,2,0:T(8,128)(2,1)}, f32[12,1024,128]{1,2,0:T(8,128)}, f32[12,1024,128]{1,...) while((s32[]{:T(128)}, bf16[12,512,128]{1,2,0:T(8,128)(2,1)}, ...), condition=%wide.region_4.5_spmd.clone, body=%wide.region_0.4_spmd.clone.sunk | while | flops 846199808 | bytes 23157908 | solution.py:77
  77.9 3.4 fusion.81
  81.3 2.5 multiply_reduce_fusion.2
  85.4 2.1 fusion.82
  87.5 2.3 fusion.84
  95.5 3.4 fusion.81
  98.9 2.4 multiply_reduce_fusion.2
  103.0 2.1 fusion.82
  105.1 2.2 fusion.84
  113.0 3.4 fusion.81
  116.4 2.4 multiply_reduce_fusion.2
  120.5 2.1 fusion.82
  122.7 2.2 fusion.84
  130.6 3.4 fusion.81
  133.9 2.4 multiply_reduce_fusion.2
  138.1 2.1 fusion.82
  140.2 2.2 fusion.84
  148.1 3.4 fusion.81
  151.5 2.4 multiply_reduce_fusion.2
  155.6 2.1 fusion.82
  157.7 2.2 fusion.84
  165.6 3.4 fusion.81
  169.0 2.4 multiply_reduce_fusion.2
  175.3 2.2 fusion.84
  183.2 3.4 fusion.81
  186.5 2.4 multiply_reduce_fusion.2
  192.8 2.2 fusion.84
  200.7 3.4 fusion.81
  204.1 2.5 multiply_reduce_fusion.2
  210.4 2.2 fusion.84
  218.3 3.4 fusion.81
  221.6 2.5 multiply_reduce_fusion.2
  227.9 2.3 fusion.84
  235.8 3.4 fusion.81
  239.2 2.5 multiply_reduce_fusion.2
  245.5 2.2 fusion.84
  253.3 3.4 fusion.81
  256.7 2.5 multiply_reduce_fusion.2
  260.9 2.1 fusion.82
  263.0 2.2 fusion.84
  270.9 3.4 fusion.81
  274.2 2.5 multiply_reduce_fusion.2
  280.5 2.2 fusion.84
  284.8 6.4 %convolution_bitcast_fusion.4 = f32[1536,1536]{0,1:T(8,128)} fusion(bf16[512,1536]{0,1:T(8,128)(2,1)} %bitcast.146, bf16[512,1536]{1,0:T(8,128)(2,1)S(1)} %copy-done), kind=kOutput, calls=%fused_computation.55 | convolution fusion | flops 2415919104 | bytes 12582912 | tf_op jit(solution)/shard_map/dot_general | solution.py:121
  291.2 9.6 %copy.47 = f32[1536,1536]{1,0:T(8,128)} copy(f32[1536,1536]{0,1:T(8,128)} %convolution_bitcast_fusion.4) | data formatting | bytes 18874368
  300.9 2.3 fusion.42
  303.2 3.0 collective-permute-start.2
  306.3 4.6 fusion.41
  310.9 61.2 %collective-permute-done.2 = f32[2,256,1536]{1,2,0:T(8,128)S(1)} collective-permute-done((f32[2,256,1536]{1,2,0:T(8,128)S(1)}, f32[2,256,1536]{1,2,0:T(8,128)S(1)}, u32[]{:S(2)}, u32[]{:S(2)}) %collective-permute-start.2) | collective-permute-done | bytes 3145760 | tf_op jit(solution)/shard_map/ppermute | solution.py:27
  372.1 2.6 pad_maximum_fusion.1
  374.7 2.7 copy-done.1
  380.3 86.8 %collective-permute-done.3 = f32[2,256,1536]{1,2,0:T(8,128)} collective-permute-done((f32[2,256,1536]{1,2,0:T(8,128)}, f32[2,256,1536]{1,2,0:T(8,128)}, u32[]{:S(2)}, u32[]{:S(2)}) %collective-permute-start.3) | collective-permute-done | bytes 3145760 | tf_op jit(solution)/shard_map/ppermute | solution.py:27
  467.2 4.9 %fusion.46 = f32[2,512,1536]{1,2,0:T(8,128)} fusion(f32[2,512,1536]{1,2,0:T(8,128)} %copy-done.1, f32[2,256,1536]{1,2,0:T(8,128)} %collective-permute-done.3), kind=kLoop, calls=%fused_computation.64 | loop fusion | flops 786432 | bytes 9437184 | tf_op jit(solution)/shard_map/scatter-add | solution.py:119
  472.1 3.2 convert.4
  476.6 2.6 copy.45
  (105 shorter events, 112.4 us)
Async XLA Ops:
  7.2 59.3 %copy-start = (bf16[512,1536]{1,0:T(8,128)(2,1)S(1)}, bf16[512,1536]{1,0:T(8,128)(2,1)}, u32[]{:S(2)}) copy-start(bf16[512,1536]{1,0:T(8,128)(2,1)} %param.15) | copy-start | bytes 4718596
  7.2 59.3 %all-gather.2.cloned.1.call-start = ((), (), s32[]{:S(2)}) async-start(), calls=%async_computation.2 | async-start | bytes 5308416 | tf_op jit(solution)/shard_map/all_gather | solution.py:104
  7.9 370.8 %reduce-scatter.7.cloned.1.call-start = ((), (), s32[]{:S(2)}) async-start(), calls=%async_computation.3 | async-start | bytes 10616832
  15.5 38.9 %collective-permute-start = (bf16[2,256,1536]{1,2,0:T(8,128)(2,1)}, bf16[2,256,1536]{1,2,0:T(8,128)(2,1)}, u32[]{:S(2)}, u32[]{:S(2)}) collective-permute-start(bf16[2,256,1536]{1,2,0:T(8,128)(2,1)} %get-tuple-element.200), channel_id=1, source_target_pairs={{0,1},{1,2},{2,3},{4,5},{5,6},{6,7},{8,9},{9,10},{10,11},{12,13},{... | collective-permute-start | bytes 4718600 | tf_op jit(solution)/shard_map/ppermute | solution.py:16
  21.7 38.1 %collective-permute-start.1 = (bf16[2,256,1536]{1,2,0:T(8,128)(2,1)}, bf16[2,256,1536]{1,2,0:T(8,128)(2,1)}, u32[]{:S(2)}, u32[]{:S(2)}) collective-permute-start(bf16[2,256,1536]{1,2,0:T(8,128)(2,1)} %get-tuple-element.201), channel_id=1, source_target_pairs={{1,0},{2,1},{3,2},{5,4},{6,5},{7,6},{9,8},{10,9},{11,10},{13,12},{... | collective-permute-start | bytes 4718600 | tf_op jit(solution)/shard_map/ppermute | solution.py:19
  300.9 179.9 %reduce-scatter.9.cloned.1.call-start = ((), (), s32[]{:S(2)}) async-start(), calls=%async_computation.4 | async-start | bytes 1474560
  300.9 71.1 %slice-start = ((s8[6291456]{0:T(1024)(128)(4,1)}), s8[4194304]{0:T(1024)(128)(4,1)S(1)}, s32[]{:S(2)}) async-start(s8[6291456]{0:T(1024)(128)(4,1)} %bitcast.129), calls=%async_computation.5 | async-start | bytes 8388608
  300.9 71.1 %slice-start.2 = ((s8[6291456]{0:T(1024)(128)(4,1)}), s8[4194304]{0:T(1024)(128)(4,1)S(1)}, s32[]{:S(2)}) async-start(s8[6291456]{0:T(1024)(128)(4,1)} %bitcast.134), calls=%async_computation.7 | async-start | bytes 8388608
  303.2 68.8 %slice-start.1 = ((s8[6291456]{0:T(1024)(128)(4,1)}), s8[2097152]{0:T(1024)(128)(4,1)S(1)}, s32[]{:S(2)}) async-start(s8[6291456]{0:T(1024)(128)(4,1)} %bitcast.129), calls=%async_computation.6 | async-start | bytes 4194304
  303.2 68.8 %slice-start.3 = ((s8[6291456]{0:T(1024)(128)(4,1)}), s8[2097152]{0:T(1024)(128)(4,1)S(1)}, s32[]{:S(2)}) async-start(s8[6291456]{0:T(1024)(128)(4,1)} %bitcast.134), calls=%async_computation.8 | async-start | bytes 4194304
  303.2 68.8 %collective-permute-start.2 = (f32[2,256,1536]{1,2,0:T(8,128)S(1)}, f32[2,256,1536]{1,2,0:T(8,128)S(1)}, u32[]{:S(2)}, u32[]{:S(2)}) collective-permute-start(f32[2,256,1536]{1,2,0:T(8,128)S(1)} %fusion.42), channel_id=1, source_target_pairs={{0,1},{1,2},{2,3},{4,5},{5,6},{6,7},{8,9},{9,10},{10,11},{12,13},{... | collective-permute-start | bytes 9437192 | tf_op jit(solution)/shard_map/ppermute | solution.py:27
  372.1 6.7 %copy-start.2 = (bf16[12,512,128]{1,2,0:T(8,128)(2,1)S(1)}, bf16[12,512,128]{1,2,0:T(8,128)(2,1)}, u32[]{:S(2)}) copy-start(bf16[12,512,128]{1,2,0:T(8,128)(2,1)} %get-tuple-element.83) | copy-start | bytes 4718596
  374.7 2.7 copy-start.1
  377.4 89.7 %collective-permute-start.3 = (f32[2,256,1536]{1,2,0:T(8,128)}, f32[2,256,1536]{1,2,0:T(8,128)}, u32[]{:S(2)}, u32[]{:S(2)}) collective-permute-start(f32[2,256,1536]{1,2,0:T(8,128)} %get-tuple-element.194), channel_id=1, source_target_pairs={{1,0},{2,1},{3,2},{5,4},{6,5},{7,6},{9,8},{10,9},{11,10},{13,12},{... | collective-permute-start | bytes 9437192 | tf_op jit(solution)/shard_map/ppermute | solution.py:27
Sparse Core Ops, SparseCore 0:
  9.9 41.6 all-gather.1
  301.0 75.5 reduce-scatter.6
  379.4 51.3 reduce-scatter.8
where the time goes:
time: 489 us; the launch traced here: 487 us
  matrix products  184 us (38%)
  waiting for transfers between devices  182 us (37%)
  other arithmetic  63.2 us (13%)
  local copies, waits for them, and re-layouts  31.5 us (6%)
  between operations  14.6 us (3%)
  starting transfers between devices  11.9 us (2%)
    ppermute x2, waiting for transfers between devices, passed_along(): return lax.ppermute(value, axis, pairs)  148 us
    dot_general x12, matrix products, one_head(): jnp.dot(probability_b, value_head, preferred_element_type=jnp.float32)  40.5 us
    dot_general x12, matrix products, one_head(): lax.dot_general(grad_head, value_head, (((1,), (1,)), ((), ())), preferre...  29.4 us
    ppermute x1, waiting for transfers between devices, extended(): lax.ppermute(lax.slice_in_dim(block, block.shape[dim] - width, None, axis...  28.1 us
    dot_general x12, matrix products, one_head(): lax.dot_general(probability_b, grad_head, (((0,), (0,)), ((), ())), prefe...  26.7 us
    dot_general x12, matrix products, one_head(): jnp.dot(grad_scores, key_head, preferred_element_type=jnp.float32)  25.3 us
    unnamed x21, local copies, waits for them, and re-layouts  25 us
    dot_general x12, matrix products, one_head(): lax.dot_general(query_head, key_head, (((1,), (1,)), ((), ())), preferred...  24.9 us
  transfers between devices with their start and end apart: 7, of which 4 were waited for; matrix products, arithmetic and copies ran while one was open for 9% of the time, Pallas kernels for 0%

commit v1 on v0

v1 whole, which is shorter than its diff:
```python
import functools

import jax
import jax.numpy as jnp
from jax import lax
from jax.experimental import pallas as pl
from jax.experimental.pallas import tpu as pltpu
from jax.sharding import PartitionSpec as P

HEADS = 12
HEAD_DIM = 128
WINDOW = 512
HALF = WINDOW // 2
GROUP = 2
COLS = GROUP * HEAD_DIM
BLOCK = HALF
INV_ROOT = HEAD_DIM ** (-0.5)
LOG2E = 1.4426950408889634
NT = (((1,), (1,)), ((), ()))
NN = (((1,), (0,)), ((), ()))
TN = (((0,), (0,)), ((), ()))


def mm(a, b, dims):
    return lax.dot_general(a, b, dims, preferred_element_type=jnp.float32)


def fill_bias(bias, length, first_row):
    for i in range(bias.shape[0]):
        shape = (BLOCK + 2 * HALF, BLOCK)
        key = lax.broadcasted_iota(jnp.int32, shape, 0)
        query = lax.broadcasted_iota(jnp.int32, shape, 1)
        key_pos = first_row + (i * BLOCK - HALF) + key
        allowed = (key >= query) & (key < query + WINDOW) & (key_pos >= 0) & (key_pos < length)
        bias[i] = jnp.where(allowed, 0.0, -1e30)


def attend(q_ref, cols, kx, vx, g, bias, att, gq_ref, gk_acc, gv_acc, length, first_row):
    blocks = bias.shape[0]
    span = BLOCK + 2 * HALF
    for hh in range(GROUP):
        hc = slice(hh * HEAD_DIM, (hh + 1) * HEAD_DIM)
        for i in range(blocks):
            rows = slice(i * BLOCK, (i + 1) * BLOCK)
            win = slice(i * BLOCK, i * BLOCK + span)
            qh = q_ref[rows, cols][:, hc]
            gh = g[rows, hc]
            kw = kx[win, hc]
            vw = vx[win, hc]
            t = mm(kw, qh, NT) * (INV_ROOT * LOG2E) + bias[i]
            top = jnp.max(t, axis=0, keepdims=True)
            e = jnp.exp2(t - top)
            total = jnp.maximum(jnp.sum(e, axis=0, keepdims=True), 1.0)
            pos = first_row + i * BLOCK + lax.broadcasted_iota(jnp.int32, (1, BLOCK), 1)
            p = e * jnp.where(pos < length, 1.0 / total, 0.0)
            pb = p.astype(jnp.bfloat16)
            att[hc, rows] = mm(vw, pb, TN).astype(jnp.bfloat16)
            dp = mm(vw, gh, NT)
            delta = jnp.sum(p * dp, axis=0, keepdims=True)
            gs = (p * (dp - delta)).astype(jnp.bfloat16)
            gq = (mm(kw, gs, TN) * INV_ROOT).T
            gq_ref[rows, pl.ds(cols.start + hh * HEAD_DIM, HEAD_DIM)] = gq.astype(jnp.bfloat16)
            gk = mm(gs, qh, NN) * INV_ROOT
            gv = mm(pb, gh, NN)
            for acc, new in ((gk_acc, gk), (gv_acc, gv)):
                if i == 0:
                    acc[win, hc] = new
                else:
                    old = slice(i * BLOCK, i * BLOCK + 2 * HALF)
                    acc[old, hc] += new[: 2 * HALF]
                    acc[i * BLOCK + 2 * HALF : i * BLOCK + span, hc] = new[2 * HALF :]


def kernel(
    len_ref, q_ref, k_ref, v_ref, go_ref, w_ref, low_ref, high_ref,
    gq_ref, own_ref, rim_ref, wg_ref,
    bias, got, kx, vx, g, att, gk_acc, gv_acc,
):
    tok = q_ref.shape[0]
    first_row = lax.axis_index("seq") * tok
    length = len_ref[0]
    fill_bias(bias, length, first_row)
    got[...] = go_ref[...].T

    def step(n, carry):
        cols = pl.ds(pl.multiple_of(n * COLS, COLS), COLS)
        for s, (x, ref) in enumerate(((kx, k_ref), (vx, v_ref))):
            x[:HALF] = low_ref[s, :, cols]
            x[HALF : HALF + tok] = ref[:, cols]
            x[HALF + tok :] = high_ref[s, :, cols]
        g[...] = mm(go_ref[...], w_ref[:, cols], NN).astype(jnp.bfloat16)
        attend(q_ref, cols, kx, vx, g, bias, att, gq_ref, gk_acc, gv_acc, length, first_row)
        for s, acc in enumerate((gk_acc, gv_acc)):
            rim_ref[0, s, :, cols] = acc[:HALF].astype(jnp.bfloat16)
            own_ref[s, :, cols] = acc[HALF : HALF + tok]
            rim_ref[1, s, :, cols] = acc[HALF + tok :].astype(jnp.bfloat16)
        wg_ref[:, cols] = mm(got[...], att[...], NT)
        return carry

    lax.fori_loop(0, q_ref.shape[1] // COLS, step, 0)


def passed_along(value, axis, by):
    devices = lax.axis_size(axis)
    pairs = [(i, i + by) for i in range(devices) if 0 <= i + by < devices]
    return lax.ppermute(value, axis, pairs)


def shards(queries, keys, values, grad_out, out_weight, lengths):
    tok, width = queries.shape
    stacked = jnp.stack([keys, values])
    low = passed_along(stacked[:, tok - HALF :], "seq", 1)
    high = passed_along(stacked[:, :HALF], "seq", -1)
    weight = lax.all_gather(out_weight, "dp", axis=0, tiled=True)
    vmem = pl.BlockSpec(memory_space=pltpu.VMEM)
    smem = pl.BlockSpec(memory_space=pltpu.SMEM)
    bf, f32 = jnp.bfloat16, jnp.float32
    grad_query, own, rim, partial = pl.pallas_call(
        kernel,
        out_shape=(
            jax.ShapeDtypeStruct((tok, width), bf),
            jax.ShapeDtypeStruct((2, tok, width), f32),
            jax.ShapeDtypeStruct((2, 2, HALF, width), bf),
            jax.ShapeDtypeStruct((weight.shape[0], width), f32),
        ),
        in_specs=[smem] + [vmem] * 7,
        out_specs=(vmem,) * 4,
        scratch_shapes=[
            pltpu.VMEM((tok // BLOCK, BLOCK + 2 * HALF, BLOCK), f32),
            pltpu.VMEM((weight.shape[0], tok), bf),
            pltpu.VMEM((tok + 2 * HALF, COLS), bf),
            pltpu.VMEM((tok + 2 * HALF, COLS), bf),
            pltpu.VMEM((tok, COLS), bf),
            pltpu.VMEM((COLS, tok), bf),
            pltpu.VMEM((tok + 2 * HALF, COLS), f32),
            pltpu.VMEM((tok + 2 * HALF, COLS), f32),
        ],
        compiler_params=pltpu.CompilerParams(vmem_limit_bytes=60 * 1024 * 1024),
        cost_estimate=pl.CostEstimate(
            flops=20_000_000_000, bytes_accessed=30_000_000, transcendentals=5_000_000
        ),
    )(lengths, queries, keys, values, grad_out, weight, low, high)
    from_right = passed_along(rim[0], "seq", -1)
    from_left = passed_along(rim[1], "seq", 1)
    own = own.at[:, :HALF].add(from_left.astype(f32))
    own = own.at[:, tok - HALF :].add(from_right.astype(f32))
    weight_grad = lax.psum_scatter(partial, "dp", scatter_dimension=0, tiled=True)
    weight_grad = lax.psum_scatter(weight_grad, "seq", scatter_dimension=0, tiled=True)
    return grad_query, own[0].astype(bf), own[1].astype(bf), weight_grad


def solution(mesh):
    rows = P(("dp", "seq"), None)
    in_specs = (rows, rows, rows, rows, P("dp", None), P("dp"))
    return jax.shard_map(
        shards, mesh=mesh, in_specs=in_specs, out_specs=(rows,) * 4, check_vma=False
    )
```

time: 489 us -> 216 us (0.44)
  matrix products: 184 us -> 0 us
  waiting for transfers between devices: 182 us -> 123 us
  other arithmetic: 63.2 us -> 13.5 us
  Pallas kernels: 0 us -> 46.1 us
  local copies, waits for them, and re-layouts: 31.5 us -> 5.65 us
    dot_general x74 -> x0, matrix products: 184 us -> none  [the longest x12 40.5 us: one_head(): jnp.dot(probability_b, value_head, preferred_element_type=jnp.float32)]
    ppermute x2 -> x4, waiting for transfers between devices: 148 us -> 32.9 us  [passed_along(): return lax.ppermute(value, axis, pairs)]
    reduce_scatter x0 -> x2, waiting for transfers between devices: none -> 88.3 us  [the longest x1 69.5 us: shards(): lax.psum_scatter(partial, 'dp', scatter_dimension=0, tiled=True)]
    pallas_call x0 -> x1, Pallas kernels: none -> 46.1 us  [shards(): pl.pallas_call(kernel, out_shape=(jax.ShapeDtypeStruct((tok, width), bf),...]
    ppermute x2 -> x0, waiting for transfers between devices: 33.4 us -> none  [the longest x1 28.1 us: extended(): lax.ppermute(lax.slice_in_dim(block, block.shape[dim] - width, None, axis...]
    unnamed x21 -> x6, local copies, waits for them, and re-layouts: 25 us -> 1.93 us
    convert_element_type x12 -> x0, other arithmetic: 20.2 us -> none  [one_head(): (probability * (grad_probs - row_delta) * inv_root).astype(jnp.bfloat16)]
    reduce_sum x12 -> x0, other arithmetic: 18.8 us -> none  [one_head(): row_total = jnp.maximum(jnp.sum(expo, axis=1, keepdims=True), 1.0)]
  transfers between devices with their start and end apart: 7 -> 7, of which waited for: 4 -> 5; matrix products, arithmetic and copies ran while one was open for 9% -> 8% of each run, Pallas kernels for 0% -> 0%
where the time goes in v1:
time: 216 us; the launch traced here: 215 us
  waiting for transfers between devices  123 us (57%)
  Pallas kernels  46.1 us (21%)
  between operations  14.4 us (7%)
  other arithmetic  13.5 us (6%)
  starting transfers between devices  12.8 us (6%)
  local copies, waits for them, and re-layouts  5.65 us (3%)
    reduce_scatter x1, waiting for transfers between devices, shards(): lax.psum_scatter(partial, 'dp', scatter_dimension=0, tiled=True)  69.5 us
    pallas_call x1, Pallas kernels, shards(): pl.pallas_call(kernel, out_shape=(jax.ShapeDtypeStruct((tok, width), bf),...  46.1 us
    ppermute x4, waiting for transfers between devices, passed_along(): return lax.ppermute(value, axis, pairs)  32.9 us
    reduce_scatter x1, waiting for transfers between devices, shards(): lax.psum_scatter(weight_grad, 'seq', scatter_dimension=0, tiled=True)  18.8 us
    ppermute x4, starting transfers between devices, passed_along(): return lax.ppermute(value, axis, pairs)  12.7 us
  transfers between devices with their start and end apart: 7, of which 5 were waited for; matrix products, arithmetic and copies ran while one was open for 8% of the time, Pallas kernels for 0%

profile of v1, /device:TPU:0, one launch (start us, length us, event | category | flops | bytes accessed | tf_op | source)
XLA Modules:
  0.0 215.5 jit_solution(10675843036249242933)
XLA Ops:
  7.2 0.0 all-gather.2.cloned.1.call-start
  7.2 0.7 all-gather.2.cloned.1.call-update
  7.9 0.0 reduce-scatter.3.cloned.1.call-start
  7.9 2.1 pad_maximum_fusion
  10.0 1.3 collective-permute-start.1
  11.3 5.7 %collective-permute-start = (bf16[2,256,1536]{2,1,0:T(8,128)(2,1)S(1)}, bf16[2,256,1536]{2,1,0:T(8,128)(2,1)S(1)}, u32[]{:S(2)}, u32[]{:S(2)}) collective-permute-start(bf16[2,256,1536]{2,1,0:T(8,128)(2,1)S(1)} %get-tuple-element.41), channel_id=1, source_target_pairs={{0,1},{1,2},{2,3},{4,5},{5,6},{6,7},{8,9},{9,10},{10,11},{12,13},{... | collective-permute-start | bytes 4718600 | tf_op jit(solution)/shard_map/ppermute | solution.py:106
  17.6 31.7 %collective-permute-done.1.high_ref = bf16[2,256,1536]{2,1,0:T(8,128)(2,1)S(1)} collective-permute-done((bf16[2,256,1536]{2,1,0:T(8,128)(2,1)S(1)}, bf16[2,256,1536]{2,1,0:T(8,128)(2,1)S(1)}, u32[]{:S(2)}, u32[]{:S(2)}) %collective-permute-start.1) | collective-permute-done | bytes 1572896 | tf_op jit(solution)/shard_map/ppermute | solution.py:106
  49.3 0.0 copy-start.1
  49.3 1.2 collective-permute-done.low_ref
  50.5 0.0 copy-start.2
  50.5 1.0 all-gather.2.cloned.1.call-done.w_ref
  51.5 0.0 copy-done.1
  51.5 0.1 copy-done.2
  51.6 46.1 %shard_map.93 = (bf16[512,1536]{1,0:T(8,128)(2,1)}, f32[2,512,1536]{2,1,0:T(8,128)}, bf16[2,2,256,1536]{3,2,1,0:T(8,128)(2,1)}, f32[1536,1536]{1,0:T(8,128)}) custom-call(s32[1]{0:T(128)S(6)} %copy.12.len_ref, bf16[512,1536]{1,0:T(8,128)(2,1)} %q_ref.1, bf16[512,1536]{1,0:T(8,128)(2,1)} %k_ref.1, bf16[512,1536]{1,0:T(8,128)(2,1)} %v_ref.1, ...), custom_call_target="tpu_custom_call" | custom-call | flops 20000000000 | bytes 30000000 | tf_op jit(solution)/shard_map/pallas_call | solution.py:118
  97.8 0.0 copy-start
  97.8 0.0 reduce-scatter.3.cloned.1.call-update
  97.8 0.0 reduce-scatter.5.cloned.1.call-start
  97.8 1.8 copy-done
  99.7 1.9 slice_bitcast_fusion.2
  101.5 4.5 %collective-permute-start.2 = (bf16[2,256,1536]{2,1,0:T(8,128)(2,1)}, bf16[2,256,1536]{2,1,0:T(8,128)(2,1)S(1)}, u32[]{:S(2)}, u32[]{:S(2)}) collective-permute-start(bf16[2,256,1536]{2,1,0:T(8,128)(2,1)} %get-tuple-element.39), channel_id=1, source_target_pairs={{0,1},{1,2},{2,3},{4,5},{5,6},{6,7},{8,9},{9,10},{10,11},{12,13},{... | collective-permute-start | bytes 4718600 | tf_op jit(solution)/shard_map/ppermute | solution.py:106
  106.0 1.3 collective-permute-start.3
  107.3 69.5 %reduce-scatter.3.cloned.1.call-done = f32[192,1536]{1,0:T(8,128)} async-done(((f32[1536,1536]{1,0:T(8,128)}), f32[192,1536]{1,0:T(8,128)}) %reduce-scatter.3.cloned.1.call-update) | async-done | bytes 1179664 | tf_op jit(solution)/shard_map/reduce_scatter | solution.py:147
  176.8 0.0 reduce-scatter.5.cloned.1.call-update
  176.9 0.0 collective-permute-done.2
  176.9 4.1 %add_dynamic-update-slice_fusion = f32[2,512,1536]{2,1,0:T(8,128)} fusion(f32[2,512,1536]{2,1,0:T(8,128)} %get-tuple-element.33, bf16[2,256,1536]{2,1,0:T(8,128)(2,1)S(1)} %collective-permute-done.2), kind=kLoop, calls=%fused_computation.4 | loop fusion | flops 1572864 | bytes 7864320 | tf_op jit(solution)/shard_map/scatter-add | solution.py:145
  180.9 0.0 collective-permute-done.3
  180.9 4.0 %fusion = f32[2,512,1536]{2,1,0:T(8,128)} fusion(f32[2,512,1536]{2,1,0:T(8,128)} %add_dynamic-update-slice_fusion, bf16[2,256,1536]{2,1,0:T(8,128)(2,1)S(1)} %collective-permute-done.3), kind=kLoop, calls=%fused_computation.1 | loop fusion | flops 1572864 | bytes 7864320 | tf_op jit(solution)/shard_map/scatter-add | solution.py:146
  185.0 3.3 %convert.4 = bf16[2,512,1536]{2,1,0:T(8,128)(2,1)S(1)} convert(f32[2,512,1536]{2,1,0:T(8,128)} %fusion) | non-fusion elementwise | flops 1572864 | bytes 9437184 | tf_op jit(solution)/shard_map/convert.1
  188.3 1.9 slice_bitcast_fusion
  190.2 18.8 %reduce-scatter.5.cloned.1.call-done = f32[48,1536]{1,0:T(8,128)} async-done(((f32[192,1536]{1,0:T(8,128)}), f32[48,1536]{1,0:T(8,128)}) %reduce-scatter.5.cloned.1.call-update) | async-done | bytes 294928 | tf_op jit(solution)/shard_map/reduce_scatter | solution.py:148
Async XLA Ops:
  7.2 44.4 %all-gather.2.cloned.1.call-start = ((), (), s32[]{:S(2)}) async-start(), calls=%async_computation.2 | async-start | bytes 5308416 | tf_op jit(solution)/shard_map/all_gather | solution.py:114
  7.9 168.9 %reduce-scatter.3.cloned.1.call-start = ((), (), s32[]{:S(2)}) async-start(), calls=%async_computation.3 | async-start | bytes 10616832 | tf_op jit(solution)/shard_map/reduce_scatter | solution.py:147
  10.0 39.3 %collective-permute-start.1 = (bf16[2,256,1536]{2,1,0:T(8,128)(2,1)S(1)}, bf16[2,256,1536]{2,1,0:T(8,128)(2,1)S(1)}, u32[]{:S(2)}, u32[]{:S(2)}) collective-permute-start(bf16[2,256,1536]{2,1,0:T(8,128)(2,1)S(1)} %get-tuple-element.40), channel_id=1, source_target_pairs={{1,0},{2,1},{3,2},{5,4},{6,5},{7,6},{9,8},{10,9},{11,10},{13,12},{... | collective-permute-start | bytes 4718600 | tf_op jit(solution)/shard_map/ppermute | solution.py:106
  11.3 39.2 %collective-permute-start = (bf16[2,256,1536]{2,1,0:T(8,128)(2,1)S(1)}, bf16[2,256,1536]{2,1,0:T(8,128)(2,1)S(1)}, u32[]{:S(2)}, u32[]{:S(2)}) collective-permute-start(bf16[2,256,1536]{2,1,0:T(8,128)(2,1)S(1)} %get-tuple-element.41), channel_id=1, source_target_pairs={{0,1},{1,2},{2,3},{4,5},{5,6},{6,7},{8,9},{9,10},{10,11},{12,13},{... | collective-permute-start | bytes 4718600 | tf_op jit(solution)/shard_map/ppermute | solution.py:106
  49.3 2.2 %copy-start.1 = (bf16[2,256,1536]{2,1,0:T(8,128)(2,1)}, bf16[2,256,1536]{2,1,0:T(8,128)(2,1)S(1)}, u32[]{:S(2)}) copy-start(bf16[2,256,1536]{2,1,0:T(8,128)(2,1)S(1)} %collective-permute-done.1.high_ref) | copy-start | bytes 4718596
  50.5 1.1 copy-start.2
  97.8 1.9 copy-start
  97.8 111.1 %reduce-scatter.5.cloned.1.call-start = ((), (), s32[]{:S(2)}) async-start(), calls=%async_computation.4 | async-start | bytes 1474560 | tf_op jit(solution)/shard_map/reduce_scatter | solution.py:148
  101.5 75.3 %collective-permute-start.2 = (bf16[2,256,1536]{2,1,0:T(8,128)(2,1)}, bf16[2,256,1536]{2,1,0:T(8,128)(2,1)S(1)}, u32[]{:S(2)}, u32[]{:S(2)}) collective-permute-start(bf16[2,256,1536]{2,1,0:T(8,128)(2,1)} %get-tuple-element.39), channel_id=1, source_target_pairs={{0,1},{1,2},{2,3},{4,5},{5,6},{6,7},{8,9},{9,10},{10,11},{12,13},{... | collective-permute-start | bytes 4718600 | tf_op jit(solution)/shard_map/ppermute | solution.py:106
  106.0 74.9 %collective-permute-start.3 = (bf16[2,256,1536]{2,1,0:T(8,128)(2,1)}, bf16[2,256,1536]{2,1,0:T(8,128)(2,1)S(1)}, u32[]{:S(2)}, u32[]{:S(2)}) collective-permute-start(bf16[2,256,1536]{2,1,0:T(8,128)(2,1)} %get-tuple-element.38), channel_id=1, source_target_pairs={{1,0},{2,1},{3,2},{5,4},{6,5},{7,6},{9,8},{10,9},{11,10},{13,12},{... | collective-permute-start | bytes 4718600 | tf_op jit(solution)/shard_map/ppermute | solution.py:106
Sparse Core Ops, SparseCore 0:
  9.9 41.6 all-gather.1
  97.9 78.8 reduce-scatter.2
  179.7 29.1 reduce-scatter.4

commit v2 on v1

--- a/solution.py
+++ b/solution.py
@@ -71,82 +71,314 @@
                     acc[i * BLOCK + 2 * HALF : i * BLOCK + span, hc] = new[2 * HALF :]
 
 
+def ring_add(index, by, count):
+    return lax.rem(index + by, count)
+
+
 def kernel(
-    len_ref, q_ref, k_ref, v_ref, go_ref, w_ref, low_ref, high_ref,
-    gq_ref, own_ref, rim_ref, wg_ref,
+    count, seq, len_ref, q_ref, k_ref, v_ref, go_ref, w_ref,
+    gq_ref, gk_ref, gv_ref, wg_ref,
     bias, got, kx, vx, g, att, gk_acc, gv_acc,
+    w_all, halo, rim, own, part, fin, piece, piece_in,
+    keeps, sends, recvs,
+    w_send, w_recv, w_pass, halo_send, halo_recv, rim_send, rim_recv,
+    red_send, red_recv, piece_send, piece_recv,
 ):
-    tok = q_ref.shape[0]
-    first_row = lax.axis_index("seq") * tok
+    tok, width = q_ref.shape
+    groups = width // COLS
+    chips = count // 2
+    stages = len(keeps)
+    depth = w_ref.shape[0]
+    dp, z = lax.axis_index("dp"), lax.axis_index("seq")
+    chip, core = lax.div(dp, 2), lax.rem(dp, 2)
+    sibling = dp + 1 - 2 * core
+    first_row = z * tok
     length = len_ref[0]
+    rows_out = wg_ref.shape[0]
+    split_seq = rows_out != depth
+
+    def copy(source, target, send_sem, recv_sem, to_dp, to_z):
+        return pltpu.make_async_remote_copy(
+            src_ref=source, dst_ref=target, send_sem=send_sem, recv_sem=recv_sem,
+            device_id=(to_dp, to_z), device_id_type=pl.DeviceIdType.MESH,
+        )
+
+    def columns(n):
+        return pl.ds(pl.multiple_of(n * COLS, COLS), COLS)
+
+    def same_core(d):
+        return 2 * ring_add(chip, d, chips) + core
+
+    def weight_copy(n, d):
+        to = sibling if d == 0 else same_core(d)
+        return copy(w_ref.at[:, columns(n)], w_all.at[n, dp], w_send.at[n, d], w_recv.at[n, dp], to, z)
+
+    def weight_from(n, block, to):
+        return copy(w_all.at[n, block], w_all.at[n, block], w_pass.at[n, 0], w_recv.at[n, block], to, z)
+
+    def weight_pass(n, d):
+        block = same_core(d)
+        return copy(
+            w_all.at[n, block], w_all.at[n, block], w_pass.at[n, d], w_recv.at[n, block], sibling, z
+        )
+
+    def halo_copy(n, side, s):
+        ref = (k_ref, v_ref)[s]
+        start = tok - HALF if side == 0 else 0
+        return copy(
+            ref.at[pl.ds(start, HALF), columns(n)], halo.at[side, s, n],
+            halo_send.at[side, s, n], halo_recv.at[side, s, n], dp, z + 1 - 2 * side,
+        )
+
+    def rim_copy(n, side, s):
+        return copy(
+            halo.at[side, s, n], rim.at[1 - side, s, n],
+            rim_send.at[side, s, n], rim_recv.at[1 - side, s, n], dp, z - 1 + 2 * side,
+        )
+
+    def reduce_copy(s, n):
+        bit = lax.rem(lax.div(dp, 2**s), 2)
+        return copy(
+            sends[s].at[n], recvs[s].at[n], red_send.at[s, n], red_recv.at[s, n],
+            dp + (1 - 2 * bit) * 2**s, z,
+        )
+
+    def piece_copy(n, d):
+        to = ring_add(z, d, seq)
+        rows = pl.ds(pl.multiple_of(to * rows_out, 16), rows_out)
+        return copy(
+            piece.at[n, rows], piece_in.at[n, z], piece_send.at[n, d], piece_recv.at[n, z], dp, to
+        )
+
+    def piece_from(n, d):
+        block = ring_add(z, d, seq)
+        rows = pl.ds(pl.multiple_of(block * rows_out, 16), rows_out)
+        return copy(
+            piece.at[n, rows], piece_in.at[n, block], piece_send.at[n, d], piece_recv.at[n, block],
+            dp, block,
+        )
+
+    has_before, has_after = z > 0, z < seq - 1
+    exists = (has_before, has_after)
+
+    barrier = pltpu.get_barrier_semaphore()
+    peers = [(sibling, z)]
+    peers += [(same_core(d), z) for d in range(1, chips)]
+    peers += [(dp, ring_add(z, d, seq)) for d in range(1, seq)]
+    for peer in peers:
+        pl.semaphore_signal(barrier, inc=1, device_id=peer, device_id_type=pl.DeviceIdType.MESH)
+    pl.semaphore_wait(barrier, len(peers))
+
+    def begin(n, carry):
+        for d in range(chips):
+            weight_copy(n, d).start()
+        for side in range(2):
+            @pl.when(exists[1 - side])
+            def _():
+                for s in range(2):
+                    halo_copy(n, side, s).start()
+        w_all[n, dp] = w_ref[:, columns(n)]
+        return carry
+
+    lax.fori_loop(0, groups, begin, 0)
+    for side in range(2):
+        @pl.when(jnp.logical_not(exists[side]))
+        def _():
+            halo[side] = jnp.zeros(halo.shape[1:], halo.dtype)
+
     fill_bias(bias, length, first_row)
     got[...] = go_ref[...].T
 
+    def pass_weight(n):
+        for d in range(1, chips):
+            weight_from(n, same_core(d), sibling).wait_recv()
+            weight_pass(n, d).start()
+
+    def reduce_stage(s, n):
+        slot = lax.rem(n, 2)
+        if s > 0:
+            reduce_copy(s - 1, n).wait_recv()
+
+        def held(i):
+            if s == 0:
+                return part[i]
+            return keeps[s - 1][slot, i] + recvs[s - 1][n, i].astype(jnp.float32)
+
+        if s == stages:
+            fin[n] = held(0)
+            if split_seq:
+                piece[n] = fin[n].astype(jnp.bfloat16)
+                for d in range(1, seq):
+                    piece_copy(n, d).start()
+            return
+        bit = lax.rem(lax.div(dp, 2**s), 2)
+        for i in range(keeps[s].shape[1]):
+            sends[s][n, i] = held(2 * i + 1 - bit).astype(jnp.bfloat16)
+            keeps[s][slot, i] = held(2 * i + bit)
+        reduce_copy(s, n).start()
+
+    def advance(n):
+        for s in range(stages, 0, -1):
+            @pl.when((n >= s) & (n - s < groups))
+            def _():
+                reduce_stage(s, n - s)
+
+    pass_weight(0)
+
     def step(n, carry):
-        cols = pl.ds(pl.multiple_of(n * COLS, COLS), COLS)
+        cols = columns(n)
+        for d in range(chips):
+            weight_from(n, same_core(d) + 1 - 2 * core, sibling).wait_recv()
+        weight = w_all[n].reshape(count * depth, COLS)
+        g[...] = mm(go_ref[...], weight, NN).astype(jnp.bfloat16)
+        for side in range(2):
+            @pl.when(exists[side])
+            def _():
+                for s in range(2):
+                    halo_copy(n, side, s).wait_recv()
         for s, (x, ref) in enumerate(((kx, k_ref), (vx, v_ref))):
-            x[:HALF] = low_ref[s, :, cols]
+            x[:HALF] = halo[0, s, n]
             x[HALF : HALF + tok] = ref[:, cols]
-            x[HALF + tok :] = high_ref[s, :, cols]
-        g[...] = mm(go_ref[...], w_ref[:, cols], NN).astype(jnp.bfloat16)
+            x[HALF + tok :] = halo[1, s, n]
         attend(q_ref, cols, kx, vx, g, bias, att, gq_ref, gk_acc, gv_acc, length, first_row)
         for s, acc in enumerate((gk_acc, gv_acc)):
-            rim_ref[0, s, :, cols] = acc[:HALF].astype(jnp.bfloat16)
-            own_ref[s, :, cols] = acc[HALF : HALF + tok]
-            rim_ref[1, s, :, cols] = acc[HALF + tok :].astype(jnp.bfloat16)
-        wg_ref[:, cols] = mm(got[...], att[...], NT)
+            halo[0, s, n] = acc[:HALF].astype(jnp.bfloat16)
+            halo[1, s, n] = acc[HALF + tok :].astype(jnp.bfloat16)
+            own[s, n] = acc[HALF : HALF + tok]
+        for side in range(2):
+            @pl.when(exists[side])
+            def _():
+                for s in range(2):
+                    rim_copy(n, side, s).start()
+
+        @pl.when(n + 1 < groups)
+        def _():
+            pass_weight(n + 1)
+
+        advance(n)
+        part[...] = mm(got[...], att[...], NT).reshape(part.shape)
+        reduce_stage(0, n)
         return carry
 
-    lax.fori_loop(0, q_ref.shape[1] // COLS, step, 0)
-
-
-def passed_along(value, axis, by):
-    devices = lax.axis_size(axis)
-    pairs = [(i, i + by) for i in range(devices) if 0 <= i + by < devices]
-    return lax.ppermute(value, axis, pairs)
+    lax.fori_loop(0, groups, step, 0)
+
+    def drain(n, carry):
+        advance(n)
+        return carry
+
+    lax.fori_loop(groups, groups + stages, drain, 0)
+
+    def finish(n, carry):
+        cols = columns(n)
+        for side in range(2):
+            rows = pl.ds(0 if side == 0 else tok - HALF, HALF)
+
+            @pl.when(exists[side])
+            def _():
+                for s in range(2):
+                    rim_copy(n, 1 - side, s).wait_recv()
+                    own[s, n, rows] += rim[side, s, n].astype(jnp.float32)
+
+        gk_ref[:, cols] = own[0, n].astype(jnp.bfloat16)
+        gv_ref[:, cols] = own[1, n].astype(jnp.bfloat16)
+        if split_seq:
+            total = fin[n, pl.ds(pl.multiple_of(z * rows_out, 16), rows_out)]
+            for d in range(1, seq):
+                piece_from(n, d).wait_recv()
+                total += piece_in[n, ring_add(z, d, seq)].astype(jnp.float32)
+            wg_ref[:, cols] = total
+        else:
+            wg_ref[:, cols] = fin[n]
+        for d in range(chips):
+            weight_copy(n, d).wait_send()
+        for d in range(1, chips):
+            weight_pass(n, d).wait_send()
+        for side in range(2):
+            @pl.when(exists[1 - side])
+            def _():
+                for s in range(2):
+                    halo_copy(n, side, s).wait_send()
+
+            @pl.when(exists[side])
+            def _():
+                for s in range(2):
+                    rim_copy(n, side, s).wait_send()
+        for s in range(stages):
+            reduce_copy(s, n).wait_send()
+        if split_seq:
+            for d in range(1, seq):
+                piece_copy(n, d).wait_send()
+        return carry
+
+    lax.fori_loop(0, groups, finish, 0)
 
 
 def shards(queries, keys, values, grad_out, out_weight, lengths):
     tok, width = queries.shape
-    stacked = jnp.stack([keys, values])
-    low = passed_along(stacked[:, tok - HALF :], "seq", 1)
-    high = passed_along(stacked[:, :HALF], "seq", -1)
-    weight = lax.all_gather(out_weight, "dp", axis=0, tiled=True)
+    depth = out_weight.shape[0]
+    count, seq = lax.axis_size("dp"), lax.axis_size("seq")
+    stages = count.bit_length() - 1
+    groups = width // COLS
+    wide = tok + 2 * HALF
+    split_seq = seq > 1 and (depth // seq) % 16 == 0
+    rows_out = depth // seq if split_seq else depth
     vmem = pl.BlockSpec(memory_space=pltpu.VMEM)
     smem = pl.BlockSpec(memory_space=pltpu.SMEM)
     bf, f32 = jnp.bfloat16, jnp.float32
-    grad_query, own, rim, partial = pl.pallas_call(
-        kernel,
+    dma = pltpu.SemaphoreType.DMA
+    halves = [count >> (s + 1) for s in range(stages)]
+    grad_query, grad_key, grad_value, weight_grad = pl.pallas_call(
+        functools.partial(kernel, count, seq),
         out_shape=(
             jax.ShapeDtypeStruct((tok, width), bf),
-            jax.ShapeDtypeStruct((2, tok, width), f32),
-            jax.ShapeDtypeStruct((2, 2, HALF, width), bf),
-            jax.ShapeDtypeStruct((weight.shape[0], width), f32),
+            jax.ShapeDtypeStruct((tok, width), bf),
+            jax.ShapeDtypeStruct((tok, width), bf),
+            jax.ShapeDtypeStruct((rows_out, width), f32),
         ),
-        in_specs=[smem] + [vmem] * 7,
+        in_specs=[smem] + [vmem] * 5,
         out_specs=(vmem,) * 4,
         scratch_shapes=[
             pltpu.VMEM((tok // BLOCK, BLOCK + 2 * HALF, BLOCK), f32),
-            pltpu.VMEM((weight.shape[0], tok), bf),
-            pltpu.VMEM((tok + 2 * HALF, COLS), bf),
-            pltpu.VMEM((tok + 2 * HALF, COLS), bf),
+            pltpu.VMEM((width, tok), bf),
+            pltpu.VMEM((wide, COLS), bf),
+            pltpu.VMEM((wide, COLS), bf),
             pltpu.VMEM((tok, COLS), bf),
             pltpu.VMEM((COLS, tok), bf),
-            pltpu.VMEM((tok + 2 * HALF, COLS), f32),
-            pltpu.VMEM((tok + 2 * HALF, COLS), f32),
+            pltpu.VMEM((wide, COLS), f32),
+            pltpu.VMEM((wide, COLS), f32),
+            pltpu.VMEM((groups, count, depth, COLS), bf),
+            pltpu.VMEM((2, 2, groups, HALF, COLS), bf),
+            pltpu.VMEM((2, 2, groups, HALF, COLS), bf),
+            pltpu.VMEM((2, groups, tok, COLS), f32),
+            pltpu.VMEM((count, depth, COLS), f32),
+            pltpu.VMEM((groups, depth, COLS), f32),
+            pltpu.VMEM((groups, depth, COLS), bf),
+            pltpu.VMEM((groups, seq, depth // seq if split_seq else 16, COLS), bf),
+            [pltpu.VMEM((2, h, depth, COLS), f32) for h in halves],
+            [pltpu.VMEM((groups, h, depth, COLS), bf) for h in halves],
+            [pltpu.VMEM((groups, h, depth, COLS), bf) for h in halves],
+            dma((groups, count // 2)),
+            dma((groups, count)),
+            dma((groups, count // 2)),
+            dma((2, 2, groups)),
+            dma((2, 2, groups)),
+            dma((2, 2, groups)),
+            dma((2, 2, groups)),
+            dma((stages, groups)),
+            dma((stages, groups)),
+            dma((groups, seq)),
+            dma((groups, seq)),
         ],
-        compiler_params=pltpu.CompilerParams(vmem_limit_bytes=60 * 1024 * 1024),
+        compiler_params=pltpu.CompilerParams(
+            vmem_limit_bytes=62 * 1024 * 1024, collective_id=0, has_side_effects=True
+        ),
         cost_estimate=pl.CostEstimate(
-            flops=20_000_000_000, bytes_accessed=30_000_000, transcendentals=5_000_000
+            flops=20_000_000_000, bytes_accessed=12_000_000, transcendentals=5_000_000
         ),
-    )(lengths, queries, keys, values, grad_out, weight, low, high)
-    from_right = passed_along(rim[0], "seq", -1)
-    from_left = passed_along(rim[1], "seq", 1)
-    own = own.at[:, :HALF].add(from_left.astype(f32))
-    own = own.at[:, tok - HALF :].add(from_right.astype(f32))
-    weight_grad = lax.psum_scatter(partial, "dp", scatter_dimension=0, tiled=True)
-    weight_grad = lax.psum_scatter(weight_grad, "seq", scatter_dimension=0, tiled=True)
-    return grad_query, own[0].astype(bf), own[1].astype(bf), weight_grad
+    )(lengths, queries, keys, values, grad_out, out_weight)
+    if not split_seq:
+        weight_grad = lax.psum_scatter(weight_grad, "seq", scatter_dimension=0, tiled=True)
+    return grad_query, grad_key, grad_value, weight_grad
 
 
 def solution(mesh):

time: 216 us -> 102 us (0.47)
  waiting for transfers between devices: 123 us -> 0 us
  Pallas kernels: 46.1 us -> 94.4 us
  other arithmetic: 13.5 us -> 0 us
  between operations: 14.4 us -> 1.3 us
  starting transfers between devices: 12.8 us -> 0 us
    reduce_scatter x2 -> x0, waiting for transfers between devices: 88.3 us -> none  [the longest x1 69.5 us: shards(): lax.psum_scatter(partial, 'dp', scatter_dimension=0, tiled=True)]
    pallas_call x1, Pallas kernels: 46.1 us -> 94.4 us  [shards(): pl.pallas_call(functools.partial(kernel, count, seq), out_shape=(jax.Shap...]
    ppermute x4 -> x0, waiting for transfers between devices: 32.9 us -> none  [passed_along(): return lax.ppermute(value, axis, pairs)]
    ppermute x4 -> x0, starting transfers between devices: 12.7 us -> none  [passed_along(): return lax.ppermute(value, axis, pairs)]
    scatter-add x2 -> x0, other arithmetic: 8.12 us -> none  [the longest x1 4.07 us: shards(): own = own.at[:, :HALF].add(from_left.astype(f32))]
    another operation x2 -> x0, other arithmetic: 5.37 us -> none
    unnamed x6 -> x10, local copies, waits for them, and re-layouts: 1.93 us -> 6.61 us
  transfers between devices with their start and end apart: 7 -> 0, of which waited for: 5 -> 0; matrix products, arithmetic and copies ran while one was open for 8% -> 0% of each run, Pallas kernels for 0% -> 0%
where the time goes in v2:
time: 102 us
  Pallas kernels  94.4 us (93%)
  local copies, waits for them, and re-layouts  6.61 us (6%)
  between operations  1.3 us (1%)
    pallas_call x1, Pallas kernels, shards(): pl.pallas_call(functools.partial(kernel, count, seq), out_shape=(jax.Shap...  94.4 us
    unnamed x10, local copies, waits for them, and re-layouts  6.61 us

profile of v2, /device:TPU:0, one launch (start us, length us, event | category | flops | bytes accessed | tf_op | source)
XLA Modules:
  0.0 102.3 jit_solution(1391378824484890045)
XLA Ops:
  1.3 94.4 %shard_map.93 = (bf16[512,1536]{1,0:T(8,128)(2,1)}, bf16[512,1536]{1,0:T(8,128)(2,1)}, bf16[512,1536]{1,0:T(8,128)(2,1)}, f32[48,1536]{1,0:T(8,128)}) custom-call(s32[1]{0:T(128)S(6)} %copy.14.len_ref, bf16[512,1536]{1,0:T(8,128)(2,1)} %q_ref.1, bf16[512,1536]{1,0:T(8,128)(2,1)} %k_ref.1, bf16[512,1536]{1,0:T(8,128)(2,1)} %v_ref.1, ...), custom_call_target="tpu_custom_call" | custom-call | flops 20000000000 | bytes 12000000 | tf_op jit(solution)/shard_map/pallas_call | solution.py:330
  95.6 0.0 copy-start.1
  95.6 2.8 %copy.15 = bf16[512,1536]{1,0:T(8,128)(2,1)} copy(bf16[512,1536]{1,0:T(8,128)(2,1)} %get-tuple-element.8) | data formatting | bytes 3145728
  98.4 0.0 copy-done.1
  98.4 0.0 copy-start
  98.4 1.1 %copy.16 = bf16[512,1536]{1,0:T(8,128)(2,1)} copy(bf16[512,1536]{1,0:T(8,128)(2,1)S(1)} %copy-done.1) | data formatting | bytes 3145728
  99.6 0.8 copy-done
  100.4 0.0 copy-start.2
  100.4 1.1 %copy.17 = bf16[512,1536]{1,0:T(8,128)(2,1)} copy(bf16[512,1536]{1,0:T(8,128)(2,1)S(1)} %copy-done) | data formatting | bytes 3145728
  101.5 0.0 copy-done.2
  101.5 0.7 copy.18
Async XLA Ops:
  95.6 2.8 %copy-start.1 = (bf16[512,1536]{1,0:T(8,128)(2,1)S(1)}, bf16[512,1536]{1,0:T(8,128)(2,1)}, u32[]{:S(2)}) copy-start(bf16[512,1536]{1,0:T(8,128)(2,1)} %get-tuple-element.9) | copy-start | bytes 4718596
  98.4 2.0 %copy-start = (bf16[512,1536]{1,0:T(8,128)(2,1)S(1)}, bf16[512,1536]{1,0:T(8,128)(2,1)}, u32[]{:S(2)}) copy-start(bf16[512,1536]{1,0:T(8,128)(2,1)} %get-tuple-element.10) | copy-start | bytes 4718596
  100.4 1.1 %copy-start.2 = (f32[48,1536]{1,0:T(8,128)S(1)}, f32[48,1536]{1,0:T(8,128)}, u32[]{:S(2)}) copy-start(f32[48,1536]{1,0:T(8,128)} %get-tuple-element.11) | copy-start | bytes 884740

commit v3 on v2

--- a/solution.py
+++ b/solution.py
@@ -35,40 +35,44 @@
         bias[i] = jnp.where(allowed, 0.0, -1e30)
 
 
-def attend(q_ref, cols, kx, vx, g, bias, att, gq_ref, gk_acc, gv_acc, length, first_row):
-    blocks = bias.shape[0]
+def forward(hh, i, q_ref, cols, kx, vx, bias, prob, att, length, first_row):
+    hc = slice(hh * HEAD_DIM, (hh + 1) * HEAD_DIM)
+    rows = slice(i * BLOCK, (i + 1) * BLOCK)
+    win = slice(i * BLOCK, i * BLOCK + BLOCK + 2 * HALF)
+    qh = q_ref[rows, cols][:, hc]
+    t = mm(kx[win, hc], qh, NT) * (INV_ROOT * LOG2E) + bias[i]
+    top = jnp.max(t, axis=0, keepdims=True)
+    e = jnp.exp2(t - top)
+    total = jnp.maximum(jnp.sum(e, axis=0, keepdims=True), 1.0)
+    pos = first_row + i * BLOCK + lax.broadcasted_iota(jnp.int32, (1, BLOCK), 1)
+    p = e * jnp.where(pos < length, 1.0 / total, 0.0)
+    prob[hh, i] = p
+    att[hc, rows] = mm(vx[win, hc], p.astype(jnp.bfloat16), TN).astype(jnp.bfloat16)
+
+
+def backward(hh, i, q_ref, cols, kx, vx, g, prob, gq_ref, gk_acc, gv_acc):
+    hc = slice(hh * HEAD_DIM, (hh + 1) * HEAD_DIM)
+    rows = slice(i * BLOCK, (i + 1) * BLOCK)
     span = BLOCK + 2 * HALF
-    for hh in range(GROUP):
-        hc = slice(hh * HEAD_DIM, (hh + 1) * HEAD_DIM)
-        for i in range(blocks):
-            rows = slice(i * BLOCK, (i + 1) * BLOCK)
-            win = slice(i * BLOCK, i * BLOCK + span)
-            qh = q_ref[rows, cols][:, hc]
-            gh = g[rows, hc]
-            kw = kx[win, hc]
-            vw = vx[win, hc]
-            t = mm(kw, qh, NT) * (INV_ROOT * LOG2E) + bias[i]
-            top = jnp.max(t, axis=0, keepdims=True)
-            e = jnp.exp2(t - top)
-            total = jnp.maximum(jnp.sum(e, axis=0, keepdims=True), 1.0)
-            pos = first_row + i * BLOCK + lax.broadcasted_iota(jnp.int32, (1, BLOCK), 1)
-            p = e * jnp.where(pos < length, 1.0 / total, 0.0)
-            pb = p.astype(jnp.bfloat16)
-            att[hc, rows] = mm(vw, pb, TN).astype(jnp.bfloat16)
-            dp = mm(vw, gh, NT)
-            delta = jnp.sum(p * dp, axis=0, keepdims=True)
-            gs = (p * (dp - delta)).astype(jnp.bfloat16)
-            gq = (mm(kw, gs, TN) * INV_ROOT).T
-            gq_ref[rows, pl.ds(cols.start + hh * HEAD_DIM, HEAD_DIM)] = gq.astype(jnp.bfloat16)
-            gk = mm(gs, qh, NN) * INV_ROOT
-            gv = mm(pb, gh, NN)
-            for acc, new in ((gk_acc, gk), (gv_acc, gv)):
-                if i == 0:
-                    acc[win, hc] = new
-                else:
-                    old = slice(i * BLOCK, i * BLOCK + 2 * HALF)
-                    acc[old, hc] += new[: 2 * HALF]
-                    acc[i * BLOCK + 2 * HALF : i * BLOCK + span, hc] = new[2 * HALF :]
+    win = slice(i * BLOCK, i * BLOCK + span)
+    qh = q_ref[rows, cols][:, hc]
+    gh = g[rows, hc]
+    kw = kx[win, hc]
+    p = prob[hh, i]
+    dp = mm(vx[win, hc], gh, NT)
+    delta = jnp.sum(p * dp, axis=0, keepdims=True)
+    gs = (p * (dp - delta)).astype(jnp.bfloat16)
+    gq = (mm(kw, gs, TN) * INV_ROOT).T
+    gq_ref[rows, pl.ds(cols.start + hh * HEAD_DIM, HEAD_DIM)] = gq.astype(jnp.bfloat16)
+    gk = mm(gs, qh, NN) * INV_ROOT
+    gv = mm(p.astype(jnp.bfloat16), gh, NN)
+    for acc, new in ((gk_acc, gk), (gv_acc, gv)):
+        if i == 0:
+            acc[win, hc] = new
+        else:
+            old = slice(i * BLOCK, i * BLOCK + 2 * HALF)
+            acc[old, hc] += new[: 2 * HALF]
+            acc[i * BLOCK + 2 * HALF : i * BLOCK + span, hc] = new[2 * HALF :]
 
 
 def ring_add(index, by, count):
@@ -78,7 +82,7 @@
 def kernel(
     count, seq, len_ref, q_ref, k_ref, v_ref, go_ref, w_ref,
     gq_ref, gk_ref, gv_ref, wg_ref,
-    bias, got, kx, vx, g, att, gk_acc, gv_acc,
+    bias, got, kx, vx, g, prob, att, gk_acc, gv_acc,
     w_all, halo, rim, own, part, fin, piece, piece_in,
     keeps, sends, recvs,
     w_send, w_recv, w_pass, halo_send, halo_recv, rim_send, rim_recv,
@@ -169,7 +173,7 @@
         pl.semaphore_signal(barrier, inc=1, device_id=peer, device_id_type=pl.DeviceIdType.MESH)
     pl.semaphore_wait(barrier, len(peers))
 
-    def begin(n, carry):
+    def begin(n):
         for d in range(chips):
             weight_copy(n, d).start()
         for side in range(2):
@@ -178,9 +182,8 @@
                 for s in range(2):
                     halo_copy(n, side, s).start()
         w_all[n, dp] = w_ref[:, columns(n)]
-        return carry
-
-    lax.fori_loop(0, groups, begin, 0)
+
+    begin(0)
     for side in range(2):
         @pl.when(jnp.logical_not(exists[side]))
         def _():
@@ -188,6 +191,7 @@
 
     fill_bias(bias, length, first_row)
     got[...] = go_ref[...].T
+    begin(1)
 
     def pass_weight(n):
         for d in range(1, chips):
@@ -217,70 +221,102 @@
             keeps[s][slot, i] = held(2 * i + bit)
         reduce_copy(s, n).start()
 
-    def advance(n):
-        for s in range(stages, 0, -1):
-            @pl.when((n >= s) & (n - s < groups))
-            def _():
-                reduce_stage(s, n - s)
+    def stage_if(s, n):
+        if s <= stages:
+            @pl.when((n >= 0) & (n < groups))
+            def _():
+                reduce_stage(s, n)
+
+    def even_stages(n):
+        for s in range(stages - stages % 2, 1, -2):
+            stage_if(s, n - s // 2)
+
+    def odd_stages(n):
+        for s in range(stages - 1 + stages % 2, 2, -2):
+            stage_if(s, n - s // 2)
+
+    def add_rims(n):
+        cols = columns(n)
+        for side in range(2):
+            rows = pl.ds(0 if side == 0 else tok - HALF, HALF)
+
+            @pl.when(exists[side])
+            def _():
+                for s in range(2):
+                    rim_copy(n, 1 - side, s).wait_recv()
+                    own[s, n, rows] += rim[side, s, n].astype(jnp.float32)
+
+        gk_ref[:, cols] = own[0, n].astype(jnp.bfloat16)
+        gv_ref[:, cols] = own[1, n].astype(jnp.bfloat16)
 
     pass_weight(0)
 
     def step(n, carry):
         cols = columns(n)
+        for side in range(2):
+            @pl.when(exists[side])
+            def _():
+                for s in range(2):
+                    halo_copy(n, side, s).wait_recv()
+
+        @pl.when(n + 2 < groups)
+        def _():
+            begin(n + 2)
+
+        for s, (x, ref) in enumerate(((kx, k_ref), (vx, v_ref))):
+            x[:HALF] = halo[0, s, n]
+            x[HALF : HALF + tok] = ref[:, cols]
+            x[HALF + tok :] = halo[1, s, n]
+        chains = [(hh, i) for hh in range(GROUP) for i in range(tok // BLOCK)]
+        for hh, i in chains:
+            forward(hh, i, q_ref, cols, kx, vx, bias, prob, att, length, first_row)
+        part[...] = mm(got[...], att[...], NT).reshape(part.shape)
+        reduce_stage(0, n)
+        even_stages(n)
         for d in range(chips):
             weight_from(n, same_core(d) + 1 - 2 * core, sibling).wait_recv()
         weight = w_all[n].reshape(count * depth, COLS)
         g[...] = mm(go_ref[...], weight, NN).astype(jnp.bfloat16)
-        for side in range(2):
-            @pl.when(exists[side])
-            def _():
-                for s in range(2):
-                    halo_copy(n, side, s).wait_recv()
-        for s, (x, ref) in enumerate(((kx, k_ref), (vx, v_ref))):
-            x[:HALF] = halo[0, s, n]
-            x[HALF : HALF + tok] = ref[:, cols]
-            x[HALF + tok :] = halo[1, s, n]
-        attend(q_ref, cols, kx, vx, g, bias, att, gq_ref, gk_acc, gv_acc, length, first_row)
+        for c, (hh, i) in enumerate(chains):
+            backward(hh, i, q_ref, cols, kx, vx, g, prob, gq_ref, gk_acc, gv_acc)
+            if c == 0:
+                reduce_stage(1, n)
+            if c == len(chains) // 2:
+                odd_stages(n)
         for s, acc in enumerate((gk_acc, gv_acc)):
             halo[0, s, n] = acc[:HALF].astype(jnp.bfloat16)
             halo[1, s, n] = acc[HALF + tok :].astype(jnp.bfloat16)
-            own[s, n] = acc[HALF : HALF + tok]
         for side in range(2):
             @pl.when(exists[side])
             def _():
                 for s in range(2):
                     rim_copy(n, side, s).start()
+
+        for s, acc in enumerate((gk_acc, gv_acc)):
+            own[s, n] = acc[HALF : HALF + tok]
 
         @pl.when(n + 1 < groups)
         def _():
             pass_weight(n + 1)
 
-        advance(n)
-        part[...] = mm(got[...], att[...], NT).reshape(part.shape)
-        reduce_stage(0, n)
+        @pl.when(n >= 2)
+        def _():
+            add_rims(n - 2)
+
         return carry
 
     lax.fori_loop(0, groups, step, 0)
 
-    def drain(n, carry):
-        advance(n)
-        return carry
-
-    lax.fori_loop(groups, groups + stages, drain, 0)
+    for late in range((stages + 1) // 2):
+        even_stages(groups + late)
+        odd_stages(groups + late)
 
     def finish(n, carry):
         cols = columns(n)
-        for side in range(2):
-            rows = pl.ds(0 if side == 0 else tok - HALF, HALF)
-
-            @pl.when(exists[side])
-            def _():
-                for s in range(2):
-                    rim_copy(n, 1 - side, s).wait_recv()
-                    own[s, n, rows] += rim[side, s, n].astype(jnp.float32)
-
-        gk_ref[:, cols] = own[0, n].astype(jnp.bfloat16)
-        gv_ref[:, cols] = own[1, n].astype(jnp.bfloat16)
+        @pl.when(n >= groups - 2)
+        def _():
+            add_rims(n)
+
         if split_seq:
             total = fin[n, pl.ds(pl.multiple_of(z * rows_out, 16), rows_out)]
             for d in range(1, seq):
@@ -311,6 +347,31 @@
         return carry
 
     lax.fori_loop(0, groups, finish, 0)
+
+
+def copy_kernel(*refs):
+    half = len(refs) // 2
+    for source, target in zip(refs[:half], refs[half:]):
+        target[...] = source[...]
+
+
+def handed_on(*arrays):
+    steps = 4 if all(x.shape[0] % 64 == 0 for x in arrays[:-1]) else 1
+
+    def spec(x):
+        rows = x.shape[0] // steps if x.shape[0] % (steps * 8) == 0 else x.shape[0]
+        whole = rows == x.shape[0]
+        return pl.BlockSpec((rows, x.shape[1]), (lambda n: (0, 0)) if whole else (lambda n: (n, 0)))
+
+    specs = [spec(x) for x in arrays]
+    return pl.pallas_call(
+        copy_kernel,
+        grid=(steps,),
+        out_shape=[jax.ShapeDtypeStruct(x.shape, x.dtype) for x in arrays],
+        in_specs=specs,
+        out_specs=specs,
+        compiler_params=pltpu.CompilerParams(vmem_limit_bytes=32 * 1024 * 1024),
+    )(*arrays)
 
 
 def shards(queries, keys, values, grad_out, out_weight, lengths):
@@ -343,6 +404,7 @@
             pltpu.VMEM((wide, COLS), bf),
             pltpu.VMEM((wide, COLS), bf),
             pltpu.VMEM((tok, COLS), bf),
+            pltpu.VMEM((GROUP, tok // BLOCK, BLOCK + 2 * HALF, BLOCK), f32),
             pltpu.VMEM((COLS, tok), bf),
             pltpu.VMEM((wide, COLS), f32),
             pltpu.VMEM((wide, COLS), f32),
@@ -378,7 +440,7 @@
     )(lengths, queries, keys, values, grad_out, out_weight)
     if not split_seq:
         weight_grad = lax.psum_scatter(weight_grad, "seq", scatter_dimension=0, tiled=True)
-    return grad_query, grad_key, grad_value, weight_grad
+    return handed_on(grad_query, grad_key, grad_value, weight_grad)
 
 
 def solution(mesh):

time: 102 us -> 104 us (1.020)
  Pallas kernels: 94.4 us -> 97.1 us
  local copies, waits for them, and re-layouts: 6.61 us -> 5.18 us
    pallas_call x0 -> x1, Pallas kernels: none -> 2.68 us  [handed_on(): pl.pallas_call(copy_kernel, grid=(steps,), out_shape=[jax.ShapeDtypeStruc...]
    unnamed x10 -> x8, local copies, waits for them, and re-layouts: 6.61 us -> 5.18 us
where the time goes in v3:
time: 104 us
  Pallas kernels  97.1 us (93%)
  local copies, waits for them, and re-layouts  5.18 us (5%)
  between operations  1.3 us (1%)
    pallas_call x1, Pallas kernels, shards(): pl.pallas_call(functools.partial(kernel, count, seq), out_shape=(jax.Shap...  94.5 us
    unnamed x8, local copies, waits for them, and re-layouts  5.18 us
    pallas_call x1, Pallas kernels, handed_on(): pl.pallas_call(copy_kernel, grid=(steps,), out_shape=[jax.ShapeDtypeStruc...  2.68 us

profile of v3, /device:TPU:0, one launch (start us, length us, event | category | flops | bytes accessed | tf_op | source)
XLA Modules:
  0.0 103.6 jit_solution(14256277290925580099)
XLA Ops:
  1.3 94.5 %shard_map.93 = (bf16[512,1536]{1,0:T(8,128)(2,1)}, bf16[512,1536]{1,0:T(8,128)(2,1)}, bf16[512,1536]{1,0:T(8,128)(2,1)}, f32[48,1536]{1,0:T(8,128)}) custom-call(s32[1]{0:T(128)S(6)} %copy.10.len_ref, bf16[512,1536]{1,0:T(8,128)(2,1)} %q_ref.1, bf16[512,1536]{1,0:T(8,128)(2,1)} %k_ref.1, bf16[512,1536]{1,0:T(8,128)(2,1)} %v_ref.1, ...), custom_call_target="tpu_custom_call" | custom-call | flops 20000000000 | bytes 12000000 | tf_op jit(solution)/shard_map/pallas_call | solution.py:391
  95.8 0.0 copy-start
  95.8 1.4 %copy-done = bf16[512,1536]{1,0:T(8,128)(2,1)S(1)} copy-done((bf16[512,1536]{1,0:T(8,128)(2,1)S(1)}, bf16[512,1536]{1,0:T(8,128)(2,1)}, u32[]{:S(2)}) %copy-start) | copy-done | bytes 1572888
  97.2 0.0 copy-start.1
  97.2 1.4 %copy-done.1 = bf16[512,1536]{1,0:T(8,128)(2,1)S(1)} copy-done((bf16[512,1536]{1,0:T(8,128)(2,1)S(1)}, bf16[512,1536]{1,0:T(8,128)(2,1)}, u32[]{:S(2)}) %copy-start.1) | copy-done | bytes 1572888
  98.6 0.0 copy-start.2
  98.6 1.4 %copy-done.2 = bf16[512,1536]{1,0:T(8,128)(2,1)S(1)} copy-done((bf16[512,1536]{1,0:T(8,128)(2,1)S(1)}, bf16[512,1536]{1,0:T(8,128)(2,1)}, u32[]{:S(2)}) %copy-start.2) | copy-done | bytes 1572888
  100.0 0.0 copy-start.3
  100.0 1.0 copy-done.3
  100.9 2.7 %shard_map.94 = (bf16[512,1536]{1,0:T(8,128)(2,1)}, bf16[512,1536]{1,0:T(8,128)(2,1)}, bf16[512,1536]{1,0:T(8,128)(2,1)}, f32[48,1536]{1,0:T(8,128)}) custom-call(bf16[512,1536]{1,0:T(8,128)(2,1)S(1)} %copy-done, bf16[512,1536]{1,0:T(8,128)(2,1)S(1)} %copy-done.1, bf16[512,1536]{1,0:T(8,128)(2,1)S(1)} %copy-done.2, f32[48,1536]{1,0:T(8,128)S(1)} %copy-done.3), custom_call_target="tpu_custom_call" | custom-call | tf_op jit(solution)/shard_map/pallas_call | solution.py:367
Async XLA Ops:
  95.8 1.4 %copy-start = (bf16[512,1536]{1,0:T(8,128)(2,1)S(1)}, bf16[512,1536]{1,0:T(8,128)(2,1)}, u32[]{:S(2)}) copy-start(bf16[512,1536]{1,0:T(8,128)(2,1)} %get-tuple-element.8.refs_0_) | copy-start | bytes 4718596
  97.2 1.4 %copy-start.1 = (bf16[512,1536]{1,0:T(8,128)(2,1)S(1)}, bf16[512,1536]{1,0:T(8,128)(2,1)}, u32[]{:S(2)}) copy-start(bf16[512,1536]{1,0:T(8,128)(2,1)} %get-tuple-element.9.refs_1_) | copy-start | bytes 4718596
  98.6 1.4 %copy-start.2 = (bf16[512,1536]{1,0:T(8,128)(2,1)S(1)}, bf16[512,1536]{1,0:T(8,128)(2,1)}, u32[]{:S(2)}) copy-start(bf16[512,1536]{1,0:T(8,128)(2,1)} %get-tuple-element.10.refs_2_) | copy-start | bytes 4718596
  100.0 1.0 copy-start.3

commit v4 on v3

--- a/solution.py
+++ b/solution.py
@@ -50,7 +50,7 @@
     att[hc, rows] = mm(vx[win, hc], p.astype(jnp.bfloat16), TN).astype(jnp.bfloat16)
 
 
-def backward(hh, i, q_ref, cols, kx, vx, g, prob, gq_ref, gk_acc, gv_acc):
+def backward(hh, i, q_ref, cols, kx, vx, g, prob, staged, n, gk_acc, gv_acc):
     hc = slice(hh * HEAD_DIM, (hh + 1) * HEAD_DIM)
     rows = slice(i * BLOCK, (i + 1) * BLOCK)
     span = BLOCK + 2 * HALF
@@ -63,7 +63,7 @@
     delta = jnp.sum(p * dp, axis=0, keepdims=True)
     gs = (p * (dp - delta)).astype(jnp.bfloat16)
     gq = (mm(kw, gs, TN) * INV_ROOT).T
-    gq_ref[rows, pl.ds(cols.start + hh * HEAD_DIM, HEAD_DIM)] = gq.astype(jnp.bfloat16)
+    staged[0, n, rows, hc] = gq.astype(jnp.bfloat16)
     gk = mm(gs, qh, NN) * INV_ROOT
     gv = mm(p.astype(jnp.bfloat16), gh, NN)
     for acc, new in ((gk_acc, gk), (gv_acc, gv)):
@@ -80,15 +80,16 @@
 
 
 def kernel(
-    count, seq, len_ref, q_ref, k_ref, v_ref, go_ref, w_ref,
-    gq_ref, gk_ref, gv_ref, wg_ref,
+    count, seq, len_ref, q_hbm, k_hbm, v_hbm, go_hbm, w_ref,
+    gq_hbm, gk_hbm, gv_hbm, wg_ref,
+    q_ref, k_ref, v_ref, go_ref, load_sem, weight_sem, staged, store_sem,
     bias, got, kx, vx, g, prob, att, gk_acc, gv_acc,
     w_all, halo, rim, own, part, fin, piece, piece_in,
     keeps, sends, recvs,
     w_send, w_recv, w_pass, halo_send, halo_recv, rim_send, rim_recv,
     red_send, red_recv, piece_send, piece_recv,
 ):
-    tok, width = q_ref.shape
+    tok, width = q_hbm.shape
     groups = width // COLS
     chips = count // 2
     stages = len(keeps)
@@ -127,7 +128,7 @@
         )
 
     def halo_copy(n, side, s):
-        ref = (k_ref, v_ref)[s]
+        ref = (k_hbm, v_hbm)[s]
         start = tok - HALF if side == 0 else 0
         return copy(
             ref.at[pl.ds(start, HALF), columns(n)], halo.at[side, s, n],
@@ -162,9 +163,22 @@
             dp, block,
         )
 
+    def load(i):
+        source = (go_hbm, q_hbm, k_hbm, v_hbm)[i]
+        return pltpu.make_async_copy(source, (go_ref, q_ref, k_ref, v_ref)[i], load_sem.at[i])
+
+    def weight_load(n):
+        return pltpu.make_async_copy(w_ref.at[:, columns(n)], w_all.at[n, dp], weight_sem.at[n])
+
+    def store(n, i):
+        target = (gq_hbm, gk_hbm, gv_hbm)[i]
+        return pltpu.make_async_copy(staged.at[i, n], target.at[:, columns(n)], store_sem.at[i, n])
+
     has_before, has_after = z > 0, z < seq - 1
     exists = (has_before, has_after)
 
+    for i in range(4):
+        load(i).start()
     barrier = pltpu.get_barrier_semaphore()
     peers = [(sibling, z)]
     peers += [(same_core(d), z) for d in range(1, chips)]
@@ -181,7 +195,7 @@
             def _():
                 for s in range(2):
                     halo_copy(n, side, s).start()
-        w_all[n, dp] = w_ref[:, columns(n)]
+        weight_load(n).start()
 
     begin(0)
     for side in range(2):
@@ -190,8 +204,12 @@
             halo[side] = jnp.zeros(halo.shape[1:], halo.dtype)
 
     fill_bias(bias, length, first_row)
+    begin(1)
+    load(0).wait()
     got[...] = go_ref[...].T
-    begin(1)
+    begin(2)
+    for i in range(1, 4):
+        load(i).wait()
 
     def pass_weight(n):
         for d in range(1, chips):
@@ -236,7 +254,6 @@
             stage_if(s, n - s // 2)
 
     def add_rims(n):
-        cols = columns(n)
         for side in range(2):
             rows = pl.ds(0 if side == 0 else tok - HALF, HALF)
 
@@ -246,8 +263,9 @@
                     rim_copy(n, 1 - side, s).wait_recv()
                     own[s, n, rows] += rim[side, s, n].astype(jnp.float32)
 
-        gk_ref[:, cols] = own[0, n].astype(jnp.bfloat16)
-        gv_ref[:, cols] = own[1, n].astype(jnp.bfloat16)
+        for s in range(2):
+            staged[1 + s, n] = own[s, n].astype(jnp.bfloat16)
+            store(n, 1 + s).start()
 
     pass_weight(0)
 
@@ -259,9 +277,9 @@
                 for s in range(2):
                     halo_copy(n, side, s).wait_recv()
 
-        @pl.when(n + 2 < groups)
+        @pl.when(n + 3 < groups)
         def _():
-            begin(n + 2)
+            begin(n + 3)
 
         for s, (x, ref) in enumerate(((kx, k_ref), (vx, v_ref))):
             x[:HALF] = halo[0, s, n]
@@ -275,10 +293,11 @@
         even_stages(n)
         for d in range(chips):
             weight_from(n, same_core(d) + 1 - 2 * core, sibling).wait_recv()
+        weight_load(n).wait()
         weight = w_all[n].reshape(count * depth, COLS)
         g[...] = mm(go_ref[...], weight, NN).astype(jnp.bfloat16)
         for c, (hh, i) in enumerate(chains):
-            backward(hh, i, q_ref, cols, kx, vx, g, prob, gq_ref, gk_acc, gv_acc)
+            backward(hh, i, q_ref, cols, kx, vx, g, prob, staged, n, gk_acc, gv_acc)
             if c == 0:
                 reduce_stage(1, n)
             if c == len(chains) // 2:
@@ -292,6 +311,7 @@
                 for s in range(2):
                     rim_copy(n, side, s).start()
 
+        store(n, 0).start()
         for s, acc in enumerate((gk_acc, gv_acc)):
             own[s, n] = acc[HALF : HALF + tok]
 
@@ -325,6 +345,8 @@
             wg_ref[:, cols] = total
         else:
             wg_ref[:, cols] = fin[n]
+        for i in range(3):
+            store(n, i).wait()
         for d in range(chips):
             weight_copy(n, d).wait_send()
         for d in range(1, chips):
@@ -370,7 +392,7 @@
         out_shape=[jax.ShapeDtypeStruct(x.shape, x.dtype) for x in arrays],
         in_specs=specs,
         out_specs=specs,
-        compiler_params=pltpu.CompilerParams(vmem_limit_bytes=32 * 1024 * 1024),
+        compiler_params=pltpu.CompilerParams(vmem_limit_bytes=62 * 1024 * 1024),
     )(*arrays)
 
 
@@ -384,6 +406,7 @@
     split_seq = seq > 1 and (depth // seq) % 16 == 0
     rows_out = depth // seq if split_seq else depth
     vmem = pl.BlockSpec(memory_space=pltpu.VMEM)
+    hbm = pl.BlockSpec(memory_space=pl.ANY)
     smem = pl.BlockSpec(memory_space=pltpu.SMEM)
     bf, f32 = jnp.bfloat16, jnp.float32
     dma = pltpu.SemaphoreType.DMA
@@ -396,9 +419,17 @@
             jax.ShapeDtypeStruct((tok, width), bf),
             jax.ShapeDtypeStruct((rows_out, width), f32),
         ),
-        in_specs=[smem] + [vmem] * 5,
-        out_specs=(vmem,) * 4,
+        in_specs=[smem] + [hbm] * 5,
+        out_specs=(hbm, hbm, hbm, vmem),
         scratch_shapes=[
+            pltpu.VMEM((tok, width), bf),
+            pltpu.VMEM((tok, width), bf),
+            pltpu.VMEM((tok, width), bf),
+            pltpu.VMEM((tok, width), bf),
+            dma((4,)),
+            dma((groups,)),
+            pltpu.VMEM((3, groups, tok, COLS), bf),
+            dma((3, groups)),
             pltpu.VMEM((tok // BLOCK, BLOCK + 2 * HALF, BLOCK), f32),
             pltpu.VMEM((width, tok), bf),
             pltpu.VMEM((wide, COLS), bf),

time: 104 us -> 97.3 us (0.936)
  local copies, waits for them, and re-layouts: 5.18 us -> 0 us
  Pallas kernels: 97.1 us -> 95.8 us
    unnamed x8 -> x0, local copies, waits for them, and re-layouts: 5.18 us -> none
    pallas_call x1, Pallas kernels: 94.5 us -> 90.4 us  [shards(): pl.pallas_call(functools.partial(kernel, count, seq), out_shape=(jax.Shap...]
    pallas_call x1, Pallas kernels: 2.68 us -> 5.35 us  [handed_on(): pl.pallas_call(copy_kernel, grid=(steps,), out_shape=[jax.ShapeDtypeStruc...]
where the time goes in v4:
time: 97.3 us; the launch traced here: 97.1 us
  Pallas kernels  95.8 us (98%)
  between operations  1.29 us (1%)
    pallas_call x1, Pallas kernels, shards(): pl.pallas_call(functools.partial(kernel, count, seq), out_shape=(jax.Shap...  90.4 us
    pallas_call x1, Pallas kernels, handed_on(): pl.pallas_call(copy_kernel, grid=(steps,), out_shape=[jax.ShapeDtypeStruc...  5.35 us

profile of v4, /device:TPU:0, one launch (start us, length us, event | category | flops | bytes accessed | tf_op | source)
XLA Modules:
  0.0 97.1 jit_solution(13838262655098478437)
XLA Ops:
  1.3 90.4 %shard_map.93 = (bf16[512,1536]{1,0:T(8,128)(2,1)}, bf16[512,1536]{1,0:T(8,128)(2,1)}, bf16[512,1536]{1,0:T(8,128)(2,1)}, f32[48,1536]{1,0:T(8,128)}) custom-call(s32[1]{0:T(128)S(6)} %copy.10.len_ref, bf16[512,1536]{1,0:T(8,128)(2,1)} %q_hbm.1, bf16[512,1536]{1,0:T(8,128)(2,1)} %k_hbm.1, bf16[512,1536]{1,0:T(8,128)(2,1)} %v_hbm.1, ...), custom_call_target="tpu_custom_call" | custom-call | flops 20000000000 | bytes 12000000 | tf_op jit(solution)/shard_map/pallas_call | solution.py:414
  91.7 5.4 %shard_map.94 = (bf16[512,1536]{1,0:T(8,128)(2,1)}, bf16[512,1536]{1,0:T(8,128)(2,1)}, bf16[512,1536]{1,0:T(8,128)(2,1)}, f32[48,1536]{1,0:T(8,128)}) custom-call(bf16[512,1536]{1,0:T(8,128)(2,1)} %get-tuple-element.8.refs_0_, bf16[512,1536]{1,0:T(8,128)(2,1)} %get-tuple-element.9.refs_1_, bf16[512,1536]{1,0:T(8,128)(2,1)} %get-tuple-element.10.refs_2_, ...), custom_call_target="tpu_custom_call" | custom-call | tf_op jit(solution)/shard_map/pallas_call | solution.py:389

commit v5 on v4

--- a/solution.py
+++ b/solution.py
@@ -84,10 +84,10 @@
     gq_hbm, gk_hbm, gv_hbm, wg_ref,
     q_ref, k_ref, v_ref, go_ref, load_sem, weight_sem, staged, store_sem,
     bias, got, kx, vx, g, prob, att, gk_acc, gv_acc,
-    w_all, halo, rim, own, part, fin, piece, piece_in,
+    w_all, halo, rim, own, part, fin,
     keeps, sends, recvs,
     w_send, w_recv, w_pass, halo_send, halo_recv, rim_send, rim_recv,
-    red_send, red_recv, piece_send, piece_recv,
+    red_send, red_recv,
 ):
     tok, width = q_hbm.shape
     groups = width // COLS
@@ -100,7 +100,7 @@
     first_row = z * tok
     length = len_ref[0]
     rows_out = wg_ref.shape[0]
-    split_seq = rows_out != depth
+    dp_stages = count.bit_length() - 1
 
     def copy(source, target, send_sem, recv_sem, to_dp, to_z):
         return pltpu.make_async_remote_copy(
@@ -135,33 +135,20 @@
             halo_send.at[side, s, n], halo_recv.at[side, s, n], dp, z + 1 - 2 * side,
         )
 
-    def rim_copy(n, side, s):
+    def rim_copy(n, side, s, hh):
+        hc = pl.ds(hh * HEAD_DIM, HEAD_DIM)
         return copy(
-            halo.at[side, s, n], rim.at[1 - side, s, n],
-            rim_send.at[side, s, n], rim_recv.at[1 - side, s, n], dp, z - 1 + 2 * side,
+            halo.at[side, s, n, :, hc], rim.at[1 - side, s, n, :, hc],
+            rim_send.at[side, s, n, hh], rim_recv.at[1 - side, s, n, hh], dp, z - 1 + 2 * side,
         )
 
+    def reduce_bit(s):
+        return lax.rem(lax.div(dp, 2**s), 2) if s < dp_stages else lax.rem(lax.div(z, 2 ** (s - dp_stages)), 2)
+
     def reduce_copy(s, n):
-        bit = lax.rem(lax.div(dp, 2**s), 2)
-        return copy(
-            sends[s].at[n], recvs[s].at[n], red_send.at[s, n], red_recv.at[s, n],
-            dp + (1 - 2 * bit) * 2**s, z,
-        )
-
-    def piece_copy(n, d):
-        to = ring_add(z, d, seq)
-        rows = pl.ds(pl.multiple_of(to * rows_out, 16), rows_out)
-        return copy(
-            piece.at[n, rows], piece_in.at[n, z], piece_send.at[n, d], piece_recv.at[n, z], dp, to
-        )
-
-    def piece_from(n, d):
-        block = ring_add(z, d, seq)
-        rows = pl.ds(pl.multiple_of(block * rows_out, 16), rows_out)
-        return copy(
-            piece.at[n, rows], piece_in.at[n, block], piece_send.at[n, d], piece_recv.at[n, block],
-            dp, block,
-        )
+        move = 1 - 2 * reduce_bit(s)
+        to = (dp + move * 2**s, z) if s < dp_stages else (dp, z + move * 2 ** (s - dp_stages))
+        return copy(sends[s].at[n], recvs[s].at[n], red_send.at[s, n], red_recv.at[s, n], *to)
 
     def load(i):
         source = (go_hbm, q_hbm, k_hbm, v_hbm)[i]
@@ -208,6 +195,7 @@
     load(0).wait()
     got[...] = go_ref[...].T
     begin(2)
+    begin(3)
     for i in range(1, 4):
         load(i).wait()
 
@@ -224,16 +212,15 @@
         def held(i):
             if s == 0:
                 return part[i]
+            if s == dp_stages < stages:
+                rows = pl.ds(pl.multiple_of(i * rows_out, 16), rows_out)
+                return keeps[s - 1][slot, 0, rows] + recvs[s - 1][n, 0, rows].astype(jnp.float32)
             return keeps[s - 1][slot, i] + recvs[s - 1][n, i].astype(jnp.float32)
 
         if s == stages:
             fin[n] = held(0)
-            if split_seq:
-                piece[n] = fin[n].astype(jnp.bfloat16)
-                for d in range(1, seq):
-                    piece_copy(n, d).start()
             return
-        bit = lax.rem(lax.div(dp, 2**s), 2)
+        bit = reduce_bit(s)
         for i in range(keeps[s].shape[1]):
             sends[s][n, i] = held(2 * i + 1 - bit).astype(jnp.bfloat16)
             keeps[s][slot, i] = held(2 * i + bit)
@@ -260,57 +247,75 @@
             @pl.when(exists[side])
             def _():
                 for s in range(2):
-                    rim_copy(n, 1 - side, s).wait_recv()
+                    for hh in range(GROUP):
+                        rim_copy(n, 1 - side, s, hh).wait_recv()
                     own[s, n, rows] += rim[side, s, n].astype(jnp.float32)
 
         for s in range(2):
             staged[1 + s, n] = own[s, n].astype(jnp.bfloat16)
             store(n, 1 + s).start()
 
+    chains = [(hh, i) for hh in range(GROUP) for i in range(tok // BLOCK)]
+
+    def ahead(n):
+        for side in range(2):
+            @pl.when(exists[side])
+            def _():
+                for s in range(2):
+                    halo_copy(n, side, s).wait_recv()
+
+        @pl.when((n >= 1) & (n + 3 < groups))
+        def _():
+            begin(n + 3)
+
+        cols = columns(n)
+        slot = lax.rem(n, 2)
+        for s, (x, ref) in enumerate(((kx, k_ref), (vx, v_ref))):
+            x[slot, :HALF] = halo[0, s, n]
+            x[slot, HALF : HALF + tok] = ref[:, cols]
+            x[slot, HALF + tok :] = halo[1, s, n]
+        kxs, vxs, probs = kx.at[slot], vx.at[slot], prob.at[slot]
+        for hh, i in chains:
+            forward(hh, i, q_ref, cols, kxs, vxs, bias, probs, att, length, first_row)
+        part[...] = mm(got[...], att[...], NT).reshape(part.shape)
+        reduce_stage(0, n)
+
+    ahead(jnp.int32(0))
     pass_weight(0)
+    reduce_stage(1, jnp.int32(0))
 
     def step(n, carry):
         cols = columns(n)
-        for side in range(2):
-            @pl.when(exists[side])
-            def _():
-                for s in range(2):
-                    halo_copy(n, side, s).wait_recv()
-
-        @pl.when(n + 3 < groups)
-        def _():
-            begin(n + 3)
-
-        for s, (x, ref) in enumerate(((kx, k_ref), (vx, v_ref))):
-            x[:HALF] = halo[0, s, n]
-            x[HALF : HALF + tok] = ref[:, cols]
-            x[HALF + tok :] = halo[1, s, n]
-        chains = [(hh, i) for hh in range(GROUP) for i in range(tok // BLOCK)]
-        for hh, i in chains:
-            forward(hh, i, q_ref, cols, kx, vx, bias, prob, att, length, first_row)
-        part[...] = mm(got[...], att[...], NT).reshape(part.shape)
-        reduce_stage(0, n)
-        even_stages(n)
+        slot = lax.rem(n, 2)
+
+        @pl.when(n + 1 < groups)
+        def _():
+            ahead(n + 1)
+
+        even_stages(n + 1)
         for d in range(chips):
             weight_from(n, same_core(d) + 1 - 2 * core, sibling).wait_recv()
         weight_load(n).wait()
         weight = w_all[n].reshape(count * depth, COLS)
         g[...] = mm(go_ref[...], weight, NN).astype(jnp.bfloat16)
         for c, (hh, i) in enumerate(chains):
-            backward(hh, i, q_ref, cols, kx, vx, g, prob, staged, n, gk_acc, gv_acc)
+            backward(
+                hh, i, q_ref, cols, kx.at[slot], vx.at[slot], g, prob.at[slot], staged, n, gk_acc, gv_acc
+            )
             if c == 0:
-                reduce_stage(1, n)
+                stage_if(1, n + 1)
             if c == len(chains) // 2:
-                odd_stages(n)
-        for s, acc in enumerate((gk_acc, gv_acc)):
-            halo[0, s, n] = acc[:HALF].astype(jnp.bfloat16)
-            halo[1, s, n] = acc[HALF + tok :].astype(jnp.bfloat16)
-        for side in range(2):
-            @pl.when(exists[side])
-            def _():
-                for s in range(2):
-                    rim_copy(n, side, s).start()
-
+                odd_stages(n + 1)
+            if i == tok // BLOCK - 1:
+                hc = slice(hh * HEAD_DIM, (hh + 1) * HEAD_DIM)
+                for s, acc in enumerate((gk_acc, gv_acc)):
+                    halo[0, s, n, :, hc] = acc[:HALF, hc].astype(jnp.bfloat16)
+                    halo[1, s, n, :, hc] = acc[HALF + tok :, hc].astype(jnp.bfloat16)
+                for side in range(2):
+                    @pl.when(exists[side])
+                    def _():
+                        for s in range(2):
+                            rim_copy(n, side, s, hh).start()
         store(n, 0).start()
         for s, acc in enumerate((gk_acc, gv_acc)):
             own[s, n] = acc[HALF : HALF + tok]
@@ -327,7 +332,7 @@
 
     lax.fori_loop(0, groups, step, 0)
 
-    for late in range((stages + 1) // 2):
+    for late in range(1, (stages + 1) // 2):
         even_stages(groups + late)
         odd_stages(groups + late)
 
@@ -337,14 +342,7 @@
         def _():
             add_rims(n)
 
-        if split_seq:
-            total = fin[n, pl.ds(pl.multiple_of(z * rows_out, 16), rows_out)]
-            for d in range(1, seq):
-                piece_from(n, d).wait_recv()
-                total += piece_in[n, ring_add(z, d, seq)].astype(jnp.float32)
-            wg_ref[:, cols] = total
-        else:
-            wg_ref[:, cols] = fin[n]
+        wg_ref[:, cols] = fin[n]
         for i in range(3):
             store(n, i).wait()
         for d in range(chips):
@@ -360,38 +358,48 @@
             @pl.when(exists[side])
             def _():
                 for s in range(2):
-                    rim_copy(n, side, s).wait_send()
+                    for hh in range(GROUP):
+                        rim_copy(n, side, s, hh).wait_send()
         for s in range(stages):
             reduce_copy(s, n).wait_send()
-        if split_seq:
-            for d in range(1, seq):
-                piece_copy(n, d).wait_send()
         return carry
 
     lax.fori_loop(0, groups, finish, 0)
 
 
 def copy_kernel(*refs):
-    half = len(refs) // 2
-    for source, target in zip(refs[:half], refs[half:]):
-        target[...] = source[...]
+    *refs, read_sem, write_sem = refs
+    third = len(refs) // 3
+    parts = []
+    for i, (source, target, held) in enumerate(zip(refs[:third], refs[third : 2 * third], refs[2 * third :])):
+        count = 4 if source.shape[0] % 64 == 0 else 1
+        size = source.shape[0] // count
+        for j in range(count):
+            rows = pl.ds(j * size, size)
+            parts.append(
+                (
+                    pltpu.make_async_copy(source.at[rows], held.at[rows], read_sem.at[i, j]),
+                    pltpu.make_async_copy(held.at[rows], target.at[rows], write_sem.at[i, j]),
+                )
+            )
+    for read, write in parts:
+        read.start()
+    for read, write in parts:
+        read.wait()
+        write.start()
+    for read, write in parts:
+        write.wait()
 
 
 def handed_on(*arrays):
-    steps = 4 if all(x.shape[0] % 64 == 0 for x in arrays[:-1]) else 1
-
-    def spec(x):
-        rows = x.shape[0] // steps if x.shape[0] % (steps * 8) == 0 else x.shape[0]
-        whole = rows == x.shape[0]
-        return pl.BlockSpec((rows, x.shape[1]), (lambda n: (0, 0)) if whole else (lambda n: (n, 0)))
-
-    specs = [spec(x) for x in arrays]
+    hbm = pl.BlockSpec(memory_space=pl.ANY)
     return pl.pallas_call(
         copy_kernel,
-        grid=(steps,),
         out_shape=[jax.ShapeDtypeStruct(x.shape, x.dtype) for x in arrays],
-        in_specs=specs,
-        out_specs=specs,
+        in_specs=[hbm] * len(arrays),
+        out_specs=[hbm] * len(arrays),
+        scratch_shapes=[pltpu.VMEM(x.shape, x.dtype) for x in arrays]
+        + [pltpu.SemaphoreType.DMA((len(arrays), 4))] * 2,
         compiler_params=pltpu.CompilerParams(vmem_limit_bytes=62 * 1024 * 1024),
     )(*arrays)
 
@@ -403,14 +411,16 @@
     stages = count.bit_length() - 1
     groups = width // COLS
     wide = tok + 2 * HALF
-    split_seq = seq > 1 and (depth // seq) % 16 == 0
+    split_seq = seq > 1 and (depth // seq) % 16 == 0 and seq & (seq - 1) == 0
     rows_out = depth // seq if split_seq else depth
     vmem = pl.BlockSpec(memory_space=pltpu.VMEM)
     hbm = pl.BlockSpec(memory_space=pl.ANY)
     smem = pl.BlockSpec(memory_space=pltpu.SMEM)
     bf, f32 = jnp.bfloat16, jnp.float32
     dma = pltpu.SemaphoreType.DMA
-    halves = [count >> (s + 1) for s in range(stages)]
+    halves = [(count >> (s + 1), depth) for s in range(stages)]
+    if split_seq:
+        halves += [(seq >> (s + 1), rows_out) for s in range(seq.bit_length() - 1)]
     grad_query, grad_key, grad_value, weight_grad = pl.pallas_call(
         functools.partial(kernel, count, seq),
         out_shape=(
@@ -432,10 +442,10 @@
             dma((3, groups)),
             pltpu.VMEM((tok // BLOCK, BLOCK + 2 * HALF, BLOCK), f32),
             pltpu.VMEM((width, tok), bf),
-            pltpu.VMEM((wide, COLS), bf),
-            pltpu.VMEM((wide, COLS), bf),
+            pltpu.VMEM((2, wide, COLS), bf),
+            pltpu.VMEM((2, wide, COLS), bf),
             pltpu.VMEM((tok, COLS), bf),
-            pltpu.VMEM((GROUP, tok // BLOCK, BLOCK + 2 * HALF, BLOCK), f32),
+            pltpu.VMEM((2, GROUP, tok // BLOCK, BLOCK + 2 * HALF, BLOCK), f32),
             pltpu.VMEM((COLS, tok), bf),
             pltpu.VMEM((wide, COLS), f32),
             pltpu.VMEM((wide, COLS), f32),
@@ -444,23 +454,19 @@
             pltpu.VMEM((2, 2, groups, HALF, COLS), bf),
             pltpu.VMEM((2, groups, tok, COLS), f32),
             pltpu.VMEM((count, depth, COLS), f32),
-            pltpu.VMEM((groups, depth, COLS), f32),
-            pltpu.VMEM((groups, depth, COLS), bf),
-            pltpu.VMEM((groups, seq, depth // seq if split_seq else 16, COLS), bf),
-            [pltpu.VMEM((2, h, depth, COLS), f32) for h in halves],
-            [pltpu.VMEM((groups, h, depth, COLS), bf) for h in halves],
-            [pltpu.VMEM((groups, h, depth, COLS), bf) for h in halves],
+            pltpu.VMEM((groups, rows_out, COLS), f32),
+            [pltpu.VMEM((2,) + h + (COLS,), f32) for h in halves],
+            [pltpu.VMEM((groups,) + h + (COLS,), bf) for h in halves],
+            [pltpu.VMEM((groups,) + h + (COLS,), bf) for h in halves],
             dma((groups, count // 2)),
             dma((groups, count)),
             dma((groups, count // 2)),
             dma((2, 2, groups)),
             dma((2, 2, groups)),
-            dma((2, 2, groups)),
-            dma((2, 2, groups)),
-            dma((stages, groups)),
-            dma((stages, groups)),
-            dma((groups, seq)),
-            dma((groups, seq)),
+            dma((2, 2, groups, GROUP)),
+            dma((2, 2, groups, GROUP)),
+            dma((len(halves), groups)),
+            dma((len(halves), groups)),
         ],
         compiler_params=pltpu.CompilerParams(
             vmem_limit_bytes=62 * 1024 * 1024, collective_id=0, has_side_effects=True

time: 97.3 us -> 106 us (1.089)
  Pallas kernels: 95.8 us -> 104 us
    pallas_call x1, Pallas kernels: 90.4 us -> 99.8 us  [shards(): pl.pallas_call(functools.partial(kernel, count, seq), out_shape=(jax.Shap...]
where the time goes in v5:
time: 106 us
  Pallas kernels  104 us (98%)
  between operations  1.45 us (1%)
    pallas_call x1, Pallas kernels, shards(): pl.pallas_call(functools.partial(kernel, count, seq), out_shape=(jax.Shap...  99.8 us
    pallas_call x1, Pallas kernels, handed_on(): pl.pallas_call(copy_kernel, out_shape=[jax.ShapeDtypeStruct(x.shape, x.dt...  4.61 us

profile of v5, /device:TPU:0, one launch (start us, length us, event | category | flops | bytes accessed | tf_op | source)
XLA Modules:
  0.0 105.9 jit_solution(5200790068271123698)
XLA Ops:
  1.3 99.8 %shard_map.93 = (bf16[512,1536]{1,0:T(8,128)(2,1)}, bf16[512,1536]{1,0:T(8,128)(2,1)}, bf16[512,1536]{1,0:T(8,128)(2,1)}, f32[48,1536]{1,0:T(8,128)}) custom-call(s32[1]{0:T(128)S(6)} %copy.10.len_ref, bf16[512,1536]{1,0:T(8,128)(2,1)} %q_hbm.1, bf16[512,1536]{1,0:T(8,128)(2,1)} %k_hbm.1, bf16[512,1536]{1,0:T(8,128)(2,1)} %v_hbm.1, ...), custom_call_target="tpu_custom_call" | custom-call | flops 20000000000 | bytes 12000000 | tf_op jit(solution)/shard_map/pallas_call | solution.py:424
  101.1 4.6 %shard_map.94 = (bf16[512,1536]{1,0:T(8,128)(2,1)}, bf16[512,1536]{1,0:T(8,128)(2,1)}, bf16[512,1536]{1,0:T(8,128)(2,1)}, f32[48,1536]{1,0:T(8,128)}) custom-call(bf16[512,1536]{1,0:T(8,128)(2,1)} %get-tuple-element.8.refs_0_, bf16[512,1536]{1,0:T(8,128)(2,1)} %get-tuple-element.9.refs_1_, bf16[512,1536]{1,0:T(8,128)(2,1)} %get-tuple-element.10.refs_2_, ...), custom_call_target="tpu_custom_call" | custom-call | tf_op jit(solution)/shard_map/pallas_call | solution.py:396

commit v6 on v4

--- a/solution.py
+++ b/solution.py
@@ -135,10 +135,11 @@
             halo_send.at[side, s, n], halo_recv.at[side, s, n], dp, z + 1 - 2 * side,
         )
 
-    def rim_copy(n, side, s):
-        return copy(
-            halo.at[side, s, n], rim.at[1 - side, s, n],
-            rim_send.at[side, s, n], rim_recv.at[1 - side, s, n], dp, z - 1 + 2 * side,
+    def rim_copy(n, side, s, hh):
+        hc = pl.ds(hh * HEAD_DIM, HEAD_DIM)
+        return copy(
+            halo.at[side, s, n, :, hc], rim.at[1 - side, s, n, :, hc],
+            rim_send.at[side, s, n, hh], rim_recv.at[1 - side, s, n, hh], dp, z - 1 + 2 * side,
         )
 
     def reduce_copy(s, n):
@@ -260,7 +261,8 @@
             @pl.when(exists[side])
             def _():
                 for s in range(2):
-                    rim_copy(n, 1 - side, s).wait_recv()
+                    for hh in range(GROUP):
+                        rim_copy(n, 1 - side, s, hh).wait_recv()
                     own[s, n, rows] += rim[side, s, n].astype(jnp.float32)
 
         for s in range(2):
@@ -300,17 +302,18 @@
             backward(hh, i, q_ref, cols, kx, vx, g, prob, staged, n, gk_acc, gv_acc)
             if c == 0:
                 reduce_stage(1, n)
+            if i == tok // BLOCK - 1:
+                hc = slice(hh * HEAD_DIM, (hh + 1) * HEAD_DIM)
+                for s, acc in enumerate((gk_acc, gv_acc)):
+                    halo[0, s, n, :, hc] = acc[:HALF, hc].astype(jnp.bfloat16)
+                    halo[1, s, n, :, hc] = acc[HALF + tok :, hc].astype(jnp.bfloat16)
+                for side in range(2):
+                    @pl.when(exists[side])
+                    def _():
+                        for s in range(2):
+                            rim_copy(n, side, s, hh).start()
             if c == len(chains) // 2:
                 odd_stages(n)
-        for s, acc in enumerate((gk_acc, gv_acc)):
-            halo[0, s, n] = acc[:HALF].astype(jnp.bfloat16)
-            halo[1, s, n] = acc[HALF + tok :].astype(jnp.bfloat16)
-        for side in range(2):
-            @pl.when(exists[side])
-            def _():
-                for s in range(2):
-                    rim_copy(n, side, s).start()
-
         store(n, 0).start()
         for s, acc in enumerate((gk_acc, gv_acc)):
             own[s, n] = acc[HALF : HALF + tok]
@@ -360,7 +363,8 @@
             @pl.when(exists[side])
             def _():
                 for s in range(2):
-                    rim_copy(n, side, s).wait_send()
+                    for hh in range(GROUP):
+                        rim_copy(n, side, s, hh).wait_send()
         for s in range(stages):
             reduce_copy(s, n).wait_send()
         if split_seq:
@@ -372,26 +376,38 @@
 
 
 def copy_kernel(*refs):
-    half = len(refs) // 2
-    for source, target in zip(refs[:half], refs[half:]):
-        target[...] = source[...]
+    *refs, read_sem, write_sem = refs
+    third = len(refs) // 3
+    parts = []
+    for i, (source, target, held) in enumerate(zip(refs[:third], refs[third : 2 * third], refs[2 * third :])):
+        count = 4 if source.shape[0] % 64 == 0 else 1
+        size = source.shape[0] // count
+        for j in range(count):
+            rows = pl.ds(j * size, size)
+            parts.append(
+                (
+                    pltpu.make_async_copy(source.at[rows], held.at[rows], read_sem.at[i, j]),
+                    pltpu.make_async_copy(held.at[rows], target.at[rows], write_sem.at[i, j]),
+                )
+            )
+    for read, write in parts:
+        read.start()
+    for read, write in parts:
+        read.wait()
+        write.start()
+    for read, write in parts:
+        write.wait()
 
 
 def handed_on(*arrays):
-    steps = 4 if all(x.shape[0] % 64 == 0 for x in arrays[:-1]) else 1
-
-    def spec(x):
-        rows = x.shape[0] // steps if x.shape[0] % (steps * 8) == 0 else x.shape[0]
-        whole = rows == x.shape[0]
-        return pl.BlockSpec((rows, x.shape[1]), (lambda n: (0, 0)) if whole else (lambda n: (n, 0)))
-
-    specs = [spec(x) for x in arrays]
+    hbm = pl.BlockSpec(memory_space=pl.ANY)
     return pl.pallas_call(
         copy_kernel,
-        grid=(steps,),
         out_shape=[jax.ShapeDtypeStruct(x.shape, x.dtype) for x in arrays],
-        in_specs=specs,
-        out_specs=specs,
+        in_specs=[hbm] * len(arrays),
+        out_specs=[hbm] * len(arrays),
+        scratch_shapes=[pltpu.VMEM(x.shape, x.dtype) for x in arrays]
+        + [pltpu.SemaphoreType.DMA((len(arrays), 4))] * 2,
         compiler_params=pltpu.CompilerParams(vmem_limit_bytes=62 * 1024 * 1024),
     )(*arrays)
 
@@ -455,8 +471,8 @@
             dma((groups, count // 2)),
             dma((2, 2, groups)),
             dma((2, 2, groups)),
-            dma((2, 2, groups)),
-            dma((2, 2, groups)),
+            dma((2, 2, groups, GROUP)),
+            dma((2, 2, groups, GROUP)),
             dma((stages, groups)),
             dma((stages, groups)),
             dma((groups, seq)),

time: 97.3 us -> 96.9 us (level)
  no operation moved by 1% of the time
where the time goes in v6:
time: 96.9 us; the launch traced here: 96.7 us
  Pallas kernels  95.5 us (99%)
  between operations  1.29 us (1%)
    pallas_call x1, Pallas kernels, shards(): pl.pallas_call(functools.partial(kernel, count, seq), out_shape=(jax.Shap...  90.9 us
    pallas_call x1, Pallas kernels, handed_on(): pl.pallas_call(copy_kernel, out_shape=[jax.ShapeDtypeStruct(x.shape, x.dt...  4.61 us

profile of v6, /device:TPU:0, one launch (start us, length us, event | category | flops | bytes accessed | tf_op | source)
XLA Modules:
  0.0 96.7 jit_solution(7219760101306154392)
XLA Ops:
  1.3 90.9 %shard_map.93 = (bf16[512,1536]{1,0:T(8,128)(2,1)}, bf16[512,1536]{1,0:T(8,128)(2,1)}, bf16[512,1536]{1,0:T(8,128)(2,1)}, f32[48,1536]{1,0:T(8,128)}) custom-call(s32[1]{0:T(128)S(6)} %copy.10.len_ref, bf16[512,1536]{1,0:T(8,128)(2,1)} %q_hbm.1, bf16[512,1536]{1,0:T(8,128)(2,1)} %k_hbm.1, bf16[512,1536]{1,0:T(8,128)(2,1)} %v_hbm.1, ...), custom_call_target="tpu_custom_call" | custom-call | flops 20000000000 | bytes 12000000 | tf_op jit(solution)/shard_map/pallas_call | solution.py:430
  92.1 4.6 %shard_map.94 = (bf16[512,1536]{1,0:T(8,128)(2,1)}, bf16[512,1536]{1,0:T(8,128)(2,1)}, bf16[512,1536]{1,0:T(8,128)(2,1)}, f32[48,1536]{1,0:T(8,128)}) custom-call(bf16[512,1536]{1,0:T(8,128)(2,1)} %get-tuple-element.8.refs_0_, bf16[512,1536]{1,0:T(8,128)(2,1)} %get-tuple-element.9.refs_1_, bf16[512,1536]{1,0:T(8,128)(2,1)} %get-tuple-element.10.refs_2_, ...), custom_call_target="tpu_custom_call" | custom-call | tf_op jit(solution)/shard_map/pallas_call | solution.py:404
